TPU v7x, 32 devices: a whole 2x2x4 slice. The times are simulated.
32 devices in a mesh: expert: 16 (over z, y, x), tensor: 2 (over core).
Axes of the slice: x: 2, y: 2, z: 4, core: 2. Of those that a mesh axis runs over, the one named last changes fastest.
Arguments:
- tokens: bfloat16 [8192, 1024], P('expert', 'tensor'), may hold values from -6 to 6
- expert_ids: int32 [8192], P('expert'), may hold values from 0 to 15, as said below
- gate_scale: float32 [8192], P('expert'), may hold values from 0.25 to 1
- gate_weight: bfloat16 [16, 1024, 6144], P('expert', None, 'tensor'), may hold values from -0.1875 to 0.1875
- up_weight: bfloat16 [16, 1024, 6144], P('expert', None, 'tensor'), may hold values from -0.1875 to 0.1875
- down_weight: bfloat16 [16, 6144, 1024], P('expert', 'tensor'), may hold values from -0.109375 to 0.109375
Outputs:
- combined: bfloat16 [8192, 1024], P('expert', 'tensor')
Inputs may be any that keep to these rules, and one draw needn't show every extreme that they name: `expert_ids`: among the 512 tokens of one index of expert, no expert id appears more than 64 times, and one expert, the same for every index, appears exactly 64 times in each.
All inputs are finite; a program needn't handle non-finite values.
Results may differ from a plain program's by a relative error of at most 0.02.
Values may be sent and summed in bfloat16 or wider, within the bound.
No kernel may reach another device: no remote copies, remote signals or barrier semaphores. Data moves between devices by JAX's collectives and lax.ppermute only.
A program may use at most 64 MiB of HBM per device.

v0:
```python
import jax
import jax.numpy as jnp
from jax import lax
from jax.sharding import PartitionSpec as P


def slot_targets(expert_ids, n_expert, capacity):
    owners = jnp.arange(n_expert, dtype=jnp.int32)
    onehot = (expert_ids[:, None] == owners[None, :]).astype(jnp.int32)
    earlier = jnp.cumsum(onehot, axis=0) - onehot
    slot_rank = jnp.sum(earlier * onehot, axis=1)
    return expert_ids * capacity + slot_rank


def shards(tokens, expert_ids, gate_scale, gate_weight, up_weight, down_weight):
    n_expert = lax.axis_size("expert")
    tok_dev = tokens.shape[0]
    capacity = 2 * tok_dev // n_expert
    slot_count = n_expert * capacity
    targets = slot_targets(expert_ids, n_expert, capacity)
    w_gate = gate_weight[0]
    w_up = up_weight[0]
    w_down = down_weight[0]
    outgoing = jnp.zeros((slot_count, tokens.shape[1]), jnp.bfloat16).at[targets].set(tokens)
    arrived = lax.all_to_all(
        outgoing.reshape(n_expert, capacity, -1), "expert", split_axis=0, concat_axis=0, tiled=True
    )
    arrived = arrived.reshape(slot_count, -1)
    piece = lax.all_gather(arrived, "tensor", axis=1, tiled=True)
    gate = jnp.dot(piece, w_gate, preferred_element_type=jnp.float32)
    up = jnp.dot(piece, w_up, preferred_element_type=jnp.float32)
    hidden = (jax.nn.silu(gate) * up).astype(jnp.bfloat16)
    partial_value = jnp.dot(hidden, w_down, preferred_element_type=jnp.float32)
    summed = lax.psum_scatter(
        partial_value.astype(jnp.bfloat16), "tensor", scatter_dimension=1, tiled=True
    )
    returned = lax.all_to_all(
        summed.reshape(n_expert, capacity, -1), "expert", split_axis=0, concat_axis=0, tiled=True
    )
    returned = returned.reshape(slot_count, -1)
    picked = returned[targets]
    return (gate_scale[:, None] * picked.astype(jnp.float32)).astype(jnp.bfloat16)


def solution(mesh):
    in_specs = (
        P("expert", "tensor"),
        P("expert"),
        P("expert"),
        P("expert", None, "tensor"),
        P("expert", None, "tensor"),
        P("expert", "tensor", None),
    )
    out_specs = P("expert", "tensor")
    return jax.shard_map(shards, mesh=mesh, in_specs=in_specs, out_specs=out_specs, check_vma=False)
```

profile of v0, /device:TPU:0, one launch (start us, length us, event | category | flops | bytes accessed | tf_op | source)
XLA Modules:
  0.0 144.6 jit_solution(10584940068104931780)
XLA Ops:
  6.5 0.0 all-gather.2.cloned.1.call-start
  6.5 0.7 fusion.17
  7.2 1.1 reduce-window.6
  8.4 0.2 slice_reduce_fusion
  8.6 0.8 fusion.16
  9.4 0.7 compare_select_fusion
  10.1 3.2 %scatter_custom_fusion = bf16[1024,512]{1,0:T(8,128)(2,1)S(1)} fusion(s32[512]{0:T(512)S(1)} %compare_select_fusion, bf16[512,512]{1,0:T(8,128)(2,1)} %param.6, bf16[]{:T(256)} %constant.5.clone.1), kind=kCustom, calls=%fused_computation.11 | custom fusion | bytes 1049088 | tf_op jit(solution)/shard_map/scatter | solution.py:24
  13.3 34.6 %all_to_all.10 = bf16[16,64,512]{2,1,0:T(8,128)(2,1)} all-to-all(bf16[16,64,512]{2,1,0:T(8,128)(2,1)S(1)} %bitcast.42), channel_id=1, replica_groups=mesh['expert'=16,'tensor'=2] {'expert'}, dimensions={0} | all-to-all | bytes 2097152 | tf_op jit(solution)/shard_map/all_to_all | solution.py:25
  47.9 0.0 all-gather.2.cloned.1.call-update
  47.9 0.2 reduce-scatter.2.cloned.1.call-start
  48.2 8.8 %all-gather.2.cloned.1.call-done = bf16[1024,1024]{1,0:T(8,128)(2,1)} async-done(((bf16[1024,512]{1,0:T(8,128)(2,1)}), bf16[1024,1024]{1,0:T(8,128)(2,1)}) %all-gather.2.cloned.1.call-update) | async-done | bytes 2097168 | tf_op jit(solution)/shard_map/all_gather | solution.py:29
  56.9 0.0 copy-start.1
  56.9 12.8 %fusion.4 = f32[1024,3072]{1,0:T(8,128)} fusion(bf16[1024,1024]{1,0:T(8,128)(2,1)} %all-gather.2.cloned.1.call-done, bf16[1,1024,3072]{2,1,0:T(8,128)(2,1)} %param.9), kind=kOutput, calls=%fused_computation.6 | convolution fusion | flops 6442450944 | bytes 20971520 | tf_op jit(solution)/shard_map/dot_general | solution.py:30
  69.7 0.0 copy-done.1
  69.7 22.7 %fusion.7 = bf16[1024,1024]{1,0:T(8,128)(2,1)} fusion(bf16[1,3072,1024]{2,1,0:T(8,128)(2,1)} %param.11, f32[1024,3072]{1,0:T(8,128)} %fusion.4, bf16[1024,1024]{1,0:T(8,128)(2,1)S(1)} %copy-done.1, bf16[1,1024,3072]{2,1,0:T(8,128)(2,1)} %param.10), kind=kOutput, calls=%fused_computation.9 | convolution fusion | flops 12904824832 | bytes 29360128 | tf_op jit(solution)/shard_map/dot_general | solution.py:33
  92.4 0.0 copy-start
  92.4 0.0 reduce-scatter.2.cloned.1.call-update
  92.5 10.9 %reduce-scatter.2.cloned.1.call-done = bf16[1024,512]{1,0:T(8,128)(2,1)} async-done(((bf16[1024,1024]{1,0:T(8,128)(2,1)}), bf16[1024,512]{1,0:T(8,128)(2,1)}) %reduce-scatter.2.cloned.1.call-update) | async-done | bytes 1048592 | tf_op jit(solution)/shard_map/reduce_scatter | solution.py:34
  103.4 6.8 %all-to-all-start.1 = ((bf16[16,64,512]{2,1,0:T(8,128)(2,1)}), bf16[16,64,512]{2,1,0:T(8,128)(2,1)S(1)}, u32[]{:S(2)}, u32[]{:S(2)}) async-start(bf16[16,64,512]{2,1,0:T(8,128)(2,1)} %bitcast.43), calls=%async_computation.2 | async-start | bytes 2097152 | tf_op jit(solution)/shard_map/all_to_all | solution.py:37
  110.2 24.6 %all-to-all-done.1 = bf16[16,64,512]{2,1,0:T(8,128)(2,1)S(1)} async-done(((bf16[16,64,512]{2,1,0:T(8,128)(2,1)}), bf16[16,64,512]{2,1,0:T(8,128)(2,1)S(1)}, u32[]{:S(2)}, u32[]{:S(2)}) %all-to-all-start.1) | async-done | bytes 1048608 | tf_op jit(solution)/shard_map/all_to_all | solution.py:37
  134.9 2.0 %gather_fusion = bf16[512,512]{1,0:T(8,128)(2,1)S(1)} fusion(bf16[1024,512]{1,0:T(8,128)(2,1)S(1)} %bitcast.40, s32[1024]{0:T(1024)S(1)} %pad_clamp_fusion), kind=kCustom, calls=%fused_computation | custom fusion | bytes 1050624 | tf_op jit(solution)/shard_map/gather | solution.py:41
  136.8 0.0 copy-done
  136.8 1.0 multiply_convert_fusion.1
  (3 shorter events, 0.0 us)
Async XLA Ops:
  6.5 50.4 %all-gather.2.cloned.1.call-start = ((), (), s32[]{:S(2)}) async-start(), calls=%async_computation.3 | async-start | bytes 3145728 | tf_op jit(solution)/shard_map/all_gather | solution.py:29
  47.9 55.5 %reduce-scatter.2.cloned.1.call-start = ((), (), s32[]{:S(2)}) async-start(), calls=%async_computation.4 | async-start | bytes 3145728 | tf_op jit(solution)/shard_map/reduce_scatter | solution.py:34
  56.9 12.8 %copy-start.1 = (bf16[1024,1024]{1,0:T(8,128)(2,1)S(1)}, bf16[1024,1024]{1,0:T(8,128)(2,1)}, u32[]{:S(2)}) copy-start(bf16[1024,1024]{1,0:T(8,128)(2,1)} %all-gather.2.cloned.1.call-done) | copy-start | bytes 6291460
  92.4 44.4 %copy-start = (f32[512]{0:T(512)S(1)}, f32[512]{0:T(512)}, u32[]{:S(2)}) copy-start(f32[512]{0:T(512)} %param.8) | copy-start | bytes 6148
  103.4 31.4 %all-to-all-start.1 = ((bf16[16,64,512]{2,1,0:T(8,128)(2,1)}), bf16[16,64,512]{2,1,0:T(8,128)(2,1)S(1)}, u32[]{:S(2)}, u32[]{:S(2)}) async-start(bf16[16,64,512]{2,1,0:T(8,128)(2,1)} %bitcast.43), calls=%async_computation.2 | async-start | bytes 2097152 | tf_op jit(solution)/shard_map/all_to_all | solution.py:37
Sparse Core Ops, SparseCore 0:
  48.0 8.8 all-gather.1
  92.6 10.7 reduce-scatter.1
where the time goes:
time: 145 us
  waiting for transfers between devices  44.4 us (31%)
  matrix products  35.5 us (24%)
  blocking collectives  34.6 us (24%)
  between operations  13.4 us (9%)
  starting transfers between devices  7.01 us (5%)
  local copies, waits for them, and re-layouts  5.41 us (4%)
  other arithmetic  4.29 us (3%)
    all_to_all x1, blocking collectives, shards(): lax.all_to_all(outgoing.reshape(n_expert, capacity, -1), 'expert', split_...  34.6 us
    all_to_all x1, waiting for transfers between devices, shards(): lax.all_to_all(summed.reshape(n_expert, capacity, -1), 'expert', split_ax...  24.6 us
    dot_general x1, matrix products, shards(): partial_value = jnp.dot(hidden, w_down, preferred_element_type=jnp.float32)  22.7 us
    dot_general x1, matrix products, shards(): gate = jnp.dot(piece, w_gate, preferred_element_type=jnp.float32)  12.8 us
    reduce_scatter x1, waiting for transfers between devices, shards(): lax.psum_scatter(partial_value.astype(jnp.bfloat16), 'tensor', scatter_di...  10.9 us
    all_gather x1, waiting for transfers between devices, shards(): piece = lax.all_gather(arrived, 'tensor', axis=1, tiled=True)  8.78 us
    all_to_all x1, starting transfers between devices, shards(): lax.all_to_all(summed.reshape(n_expert, capacity, -1), 'expert', split_ax...  6.79 us
    scatter x1, local copies, waits for them, and re-layouts, shards(): jnp.zeros((slot_count, tokens.shape[1]), jnp.bfloat16).at[targets]  3.22 us
  transfers between devices with their start and end apart: 3, of which 3 were waited for; matrix products, arithmetic and copies ran while one was open for 0% of the time, Pallas kernels for 0%

commit v1 on v0

v1 whole, which is shorter than its diff:
```python
import functools

import jax
import jax.numpy as jnp
from jax import lax
from jax.experimental import pallas as pl
from jax.experimental.pallas import tpu as pltpu
from jax.sharding import PartitionSpec as P

F32 = jnp.float32
BF16 = jnp.bfloat16
MIB = 1 << 20


def vmem():
    return pl.BlockSpec(memory_space=pltpu.VMEM)


def params(limit_mib):
    return pltpu.CompilerParams(vmem_limit_bytes=limit_mib * MIB)


def chunk_sizes(capacity):
    if capacity >= 32:
        return (capacity // 2, capacity // 2)
    return (capacity,)


def dispatch_kernel(n_expert, chunks, ids_ref, tok_ref, *out_refs):
    n_tok = tok_ref.shape[0]
    ids = ids_ref[...]
    owner = lax.broadcasted_iota(jnp.int32, (n_expert, n_tok), 0)
    onehot = (owner == ids).astype(F32)
    before = lax.broadcasted_iota(jnp.int32, (n_tok, n_tok), 0) < lax.broadcasted_iota(jnp.int32, (n_tok, n_tok), 1)
    earlier = jnp.dot(onehot.astype(BF16), before.astype(F32).astype(BF16), preferred_element_type=F32)
    rank = jnp.sum(earlier * onehot, axis=0, keepdims=True).astype(jnp.int32)
    low = 0
    for size, out_ref in zip(chunks, out_refs):
        inside = (rank >= low) & (rank < low + size)
        target = jnp.where(inside, ids * size + (rank - low), -1)
        slot = lax.broadcasted_iota(jnp.int32, (n_expert * size, n_tok), 0)
        pick = (slot == target).astype(F32).astype(BF16)
        out_ref[...] = jnp.dot(pick, tok_ref[...], preferred_element_type=F32).astype(BF16)
        low += size


def dispatch(ids, tokens, n_expert, chunks):
    n_tok, width = tokens.shape
    return pl.pallas_call(
        functools.partial(dispatch_kernel, n_expert, chunks),
        out_shape=[jax.ShapeDtypeStruct((n_expert * size, width), BF16) for size in chunks],
        in_specs=[vmem(), vmem()],
        out_specs=[vmem() for _ in chunks],
        compiler_params=params(24),
        name="dispatch",
    )(ids.reshape(1, n_tok), tokens)


def combine_map_kernel(n_expert, chunks, ids_ref, *out_refs):
    n_tok = ids_ref.shape[0]
    ids = ids_ref[...]
    owner = lax.broadcasted_iota(jnp.int32, (n_tok, n_expert), 1)
    onehot = (owner == ids).astype(F32)
    before = lax.broadcasted_iota(jnp.int32, (n_tok, n_tok), 1) < lax.broadcasted_iota(jnp.int32, (n_tok, n_tok), 0)
    earlier = jnp.dot(before.astype(F32).astype(BF16), onehot.astype(BF16), preferred_element_type=F32)
    rank = jnp.sum(earlier * onehot, axis=1, keepdims=True).astype(jnp.int32)
    low = 0
    for size, out_ref in zip(chunks, out_refs):
        inside = (rank >= low) & (rank < low + size)
        target = jnp.where(inside, ids * size + (rank - low), -1)
        slot = lax.broadcasted_iota(jnp.int32, (n_tok, n_expert * size), 1)
        out_ref[...] = (slot == target).astype(F32).astype(BF16)
        low += size


def combine_map(ids, n_expert, chunks):
    n_tok = ids.shape[0]
    return pl.pallas_call(
        functools.partial(combine_map_kernel, n_expert, chunks),
        out_shape=[jax.ShapeDtypeStruct((n_tok, n_expert * size), BF16) for size in chunks],
        in_specs=[vmem()],
        out_specs=[vmem() for _ in chunks],
        compiler_params=params(24),
        name="combine_map",
    )(ids.reshape(n_tok, 1))


def pick_kernel(map_ref, back_ref, out_ref):
    out_ref[...] = jnp.dot(map_ref[...], back_ref[...], preferred_element_type=F32).astype(BF16)


def pick(pick_map, back):
    return pl.pallas_call(
        pick_kernel,
        out_shape=jax.ShapeDtypeStruct((pick_map.shape[0], back.shape[1]), BF16),
        in_specs=[vmem(), vmem()],
        out_specs=vmem(),
        compiler_params=params(16),
        name="pick",
    )(pick_map, back)


def finish_kernel(n_part, map_ref, back_ref, scale_ref, *refs):
    total = jnp.dot(map_ref[...], back_ref[...], preferred_element_type=F32)
    for part_ref in refs[:n_part]:
        total = total + part_ref[...].astype(F32)
    refs[n_part][...] = (scale_ref[...] * total).astype(BF16)


def finish(pick_map, back, scale, parts):
    n_tok = pick_map.shape[0]
    return pl.pallas_call(
        functools.partial(finish_kernel, len(parts)),
        out_shape=jax.ShapeDtypeStruct((n_tok, back.shape[1]), BF16),
        in_specs=[vmem() for _ in range(3 + len(parts))],
        out_specs=vmem(),
        compiler_params=params(16),
        name="finish",
    )(pick_map, back, scale.reshape(n_tok, 1), *parts)


def expert_kernel(n_tensor, n_block, where_ref, *refs):
    part_refs = refs[:n_tensor]
    sources = refs[n_tensor:n_tensor + 3]
    out_refs = refs[n_tensor + 3:2 * n_tensor + 3]
    total_refs = refs[2 * n_tensor + 3:3 * n_tensor + 3]
    gate_ref, up_ref, down_ref, arrived = refs[3 * n_tensor + 3:]
    ring, _, block = gate_ref.shape
    width = part_refs[0].shape[1]
    me = where_ref[0]

    def columns(shift):
        return pl.ds(pl.multiple_of(lax.rem(me + shift, n_tensor) * width, width), width)

    def fetches(step):
        slot = lax.rem(step, ring)
        cut = pl.ds(pl.multiple_of(step * block, block), block)
        return [
            pltpu.make_async_copy(sources[0].at[0, :, cut], gate_ref.at[slot], arrived.at[slot, 0]),
            pltpu.make_async_copy(sources[1].at[0, :, cut], up_ref.at[slot], arrived.at[slot, 1]),
            pltpu.make_async_copy(sources[2].at[0, cut, :], down_ref.at[slot], arrived.at[slot, 2]),
        ]

    def start(step):
        for fetch in fetches(step):
            fetch.start()

    def product(weight_ref, slot):
        total = None
        for shift, part_ref in enumerate(part_refs):
            term = jnp.dot(part_ref[...], weight_ref[slot, columns(shift), :], preferred_element_type=F32)
            total = term if total is None else total + term
        return total

    def work(step, first):
        gate_here, up_here, down_here = fetches(step)
        slot = lax.rem(step, ring)
        gate_here.wait()
        gate = product(gate_ref, slot)
        up_here.wait()
        up = product(up_ref, slot)
        hidden = (gate / (1.0 + jnp.exp(-gate)) * up).astype(BF16)
        down_here.wait()
        for shift, total_ref in enumerate(total_refs):
            share = jnp.dot(hidden, down_ref[slot, :, columns(shift)], preferred_element_type=F32)
            if first:
                total_ref[...] = share
            else:
                total_ref[...] += share

    for step in range(min(ring, n_block)):
        start(step)
    if UNROLL:
        for step in range(n_block):
            work(step, step == 0)
            if step + ring < n_block:
                start(step + ring)
    else:
        for total_ref in total_refs:
            total_ref[...] = jnp.zeros_like(total_ref)

        @pl.loop(0, n_block)
        def _(step):
            work(step, False)

            @pl.when(step + ring < n_block)
            def _():
                start(step + ring)
    for total_ref, out_ref in zip(total_refs, out_refs):
        out_ref[...] = total_ref[...].astype(BF16)


BLOCK = 1024
RING = 2
UNROLL = False
LIMIT = 24


def expert_rows(where, parts, weights):
    n_tensor = len(parts)
    rows, width = parts[0].shape
    depth, hidden = weights[0].shape[1:]
    block = BLOCK if hidden % BLOCK == 0 else 256
    n_block = hidden // block
    ring = min(RING, n_block)
    hbm = pl.BlockSpec(memory_space=pltpu.HBM)
    return pl.pallas_call(
        functools.partial(expert_kernel, n_tensor, n_block),
        out_shape=[jax.ShapeDtypeStruct((rows, width), BF16) for _ in parts],
        in_specs=[pl.BlockSpec(memory_space=pltpu.SMEM)] + [vmem() for _ in parts] + [hbm, hbm, hbm],
        out_specs=[vmem() for _ in parts],
        scratch_shapes=[pltpu.VMEM((rows, width), F32) for _ in parts]
        + [
            pltpu.VMEM((ring, depth, block), BF16),
            pltpu.VMEM((ring, depth, block), BF16),
            pltpu.VMEM((ring, block, depth), BF16),
            pltpu.SemaphoreType.DMA((ring, 3)),
        ],
        compiler_params=params(LIMIT),
        cost_estimate=pl.CostEstimate(
            flops=6 * rows * depth * hidden, bytes_accessed=6 * depth * hidden, transcendentals=rows * hidden
        ),
        name="expert_rows",
    )(where, *parts, *[pltpu.with_memory_space_constraint(weight, pltpu.HBM) for weight in weights])


def add_kernel(*refs):
    total = refs[0][...].astype(F32)
    for ref in refs[1:-1]:
        total = total + ref[...].astype(F32)
    refs[-1][...] = total.astype(BF16)


def add(shares):
    return pl.pallas_call(
        add_kernel,
        out_shape=jax.ShapeDtypeStruct(shares[0].shape, BF16),
        in_specs=[vmem() for _ in shares],
        out_specs=vmem(),
        compiler_params=params(8),
        name="add_shares",
    )(*shares)


def order_swap(n_expert):
    return n_expert // 4 if n_expert & (n_expert - 1) == 0 else 0


def exchange(rows, n_expert):
    size = rows.shape[0] // n_expert
    swap = order_swap(n_expert)
    moved = lax.all_to_all(
        rows.reshape(n_expert, size, -1),
        "expert",
        split_axis=0,
        concat_axis=0,
        axis_index_groups=[[j ^ swap for j in range(n_expert)]],
        tiled=True,
    )
    return moved.reshape(rows.shape)


def shards(tokens, expert_ids, gate_scale, gate_weight, up_weight, down_weight):
    n_expert = lax.axis_size("expert")
    n_tensor = lax.axis_size("tensor")
    chunks = chunk_sizes(2 * tokens.shape[0] // n_expert)
    where = lax.axis_index("tensor").astype(jnp.int32).reshape(1)

    def shifted(rows, shift):
        return lax.ppermute(rows, "tensor", [(i, (i - shift) % n_tensor) for i in range(n_tensor)])

    expert_ids = expert_ids ^ order_swap(n_expert)
    outgoing = dispatch(expert_ids, tokens, n_expert, chunks)
    maps = combine_map(expert_ids, n_expert, chunks)
    weights = (gate_weight, up_weight, down_weight)
    backs = []
    for rows in outgoing:
        arrived = exchange(rows, n_expert)
        parts = [arrived] + [shifted(arrived, shift) for shift in range(1, n_tensor)]
        shares = expert_rows(where, parts, weights)
        total = add([shares[0]] + [shifted(shares[shift], -shift) for shift in range(1, n_tensor)])
        backs.append(exchange(total, n_expert))
    picked = [pick(pick_map, back) for pick_map, back in zip(maps[:-1], backs[:-1])]
    return finish(maps[-1], backs[-1], gate_scale, picked)


def solution(mesh):
    in_specs = (
        P("expert", "tensor"),
        P("expert"),
        P("expert"),
        P("expert", None, "tensor"),
        P("expert", None, "tensor"),
        P("expert", "tensor", None),
    )
    out_specs = P("expert", "tensor")
    return jax.shard_map(shards, mesh=mesh, in_specs=in_specs, out_specs=out_specs, check_vma=False)
```

time: 145 us -> 91 us (0.63)
  matrix products: 35.5 us -> 0 us
  Pallas kernels: 0 us -> 33 us
  waiting for transfers between devices: 44.4 us -> 16.5 us
  between operations: 13.4 us -> 0.1 us
  blocking collectives: 34.6 us -> 22.7 us
  starting transfers between devices: 7.01 us -> 16.2 us
  local copies, waits for them, and re-layouts: 5.41 us -> 1.33 us
  other arithmetic: 4.29 us -> 0.68 us
    dot_general x2 -> x0, matrix products: 35.5 us -> none  [the longest x1 22.7 us: shards(): partial_value = jnp.dot(hidden, w_down, preferred_element_type=jnp.float32)]
    pallas_call x0 -> x8, Pallas kernels: none -> 33 us  [the longest x2 26.8 us: expert_rows(): pl.pallas_call(functools.partial(expert_kernel, n_tensor, n_block), out_s...]
    all_to_all x1, blocking collectives: 34.6 us -> 22.7 us  [exchange(): lax.all_to_all(rows.reshape(n_expert, size, -1), 'expert', split_axis=0,...]
    reduce_scatter x1 -> x0, waiting for transfers between devices: 10.9 us -> none  [shards(): lax.psum_scatter(partial_value.astype(jnp.bfloat16), 'tensor', scatter_di...]
    all_to_all x1 -> x3, waiting for transfers between devices: 24.6 us -> 14 us  [exchange(): lax.all_to_all(rows.reshape(n_expert, size, -1), 'expert', split_axis=0,...]
    all_to_all x1 -> x3, starting transfers between devices: 6.79 us -> 16 us  [exchange(): lax.all_to_all(rows.reshape(n_expert, size, -1), 'expert', split_axis=0,...]
    all_gather x1 -> x0, waiting for transfers between devices: 8.78 us -> none  [shards(): piece = lax.all_gather(arrived, 'tensor', axis=1, tiled=True)]
    scatter x1 -> x0, local copies, waits for them, and re-layouts: 3.22 us -> none  [shards(): jnp.zeros((slot_count, tokens.shape[1]), jnp.bfloat16).at[targets]]
  transfers between devices with their start and end apart: 3 -> 7, of which waited for: 3 -> 4; matrix products, arithmetic and copies ran while one was open for 0% -> 0% of each run, Pallas kernels for 0% -> 33%
where the time goes in v1:
time: 91 us; the launch traced here: 90.5 us
  Pallas kernels  33 us (36%)
  blocking collectives  22.7 us (25%)
  waiting for transfers between devices  16.5 us (18%)
  starting transfers between devices  16.2 us (18%)
  local copies, waits for them, and re-layouts  1.33 us (1%)
    pallas_call x2, Pallas kernels, expert_rows(): pl.pallas_call(functools.partial(expert_kernel, n_tensor, n_block), out_s...  26.8 us
    all_to_all x1, blocking collectives, exchange(): lax.all_to_all(rows.reshape(n_expert, size, -1), 'expert', split_axis=0,...  22.7 us
    all_to_all x3, starting transfers between devices, exchange(): lax.all_to_all(rows.reshape(n_expert, size, -1), 'expert', split_axis=0,...  16 us
    all_to_all x3, waiting for transfers between devices, exchange(): lax.all_to_all(rows.reshape(n_expert, size, -1), 'expert', split_axis=0,...  14 us
    ppermute x4, waiting for transfers between devices, shifted(): lax.ppermute(rows, 'tensor', [(i, (i - shift) % n_tensor) for i in range(...  2.51 us
    pallas_call x2, Pallas kernels, add(): pl.pallas_call(add_kernel, out_shape=jax.ShapeDtypeStruct(shares[0].shape...  1.82 us
  transfers between devices with their start and end apart: 7, of which 4 were waited for; matrix products, arithmetic and copies ran while one was open for 0% of the time, Pallas kernels for 33%

profile of v1, /device:TPU:0, one launch (start us, length us, event | category | flops | bytes accessed | tf_op | source)
XLA Modules:
  0.0 90.5 jit_solution(18081591308033878368)
XLA Ops:
  0.0 0.7 broadcast_xor_fusion
  0.7 0.0 copy-start
  0.7 1.0 %copy-done = bf16[512,512]{1,0:T(8,128)(2,1)S(1)} copy-done((bf16[512,512]{1,0:T(8,128)(2,1)S(1)}, bf16[512,512]{1,0:T(8,128)(2,1)}, u32[]{:S(2)}) %copy-start) | copy-done | bytes 524312
  1.7 1.7 %dispatch.1 = (bf16[512,512]{1,0:T(8,128)(2,1)S(1)}, bf16[512,512]{1,0:T(8,128)(2,1)}) custom-call(s32[1,512]{1,0:T(1,128)S(1)} %bitcast.19, bf16[512,512]{1,0:T(8,128)(2,1)S(1)} %copy-done), custom_call_target="tpu_custom_call" | custom-call | tf_op jit(solution)/shard_map/dispatch/pallas_call | solution.py:49
  3.4 22.7 %all_to_all.20 = bf16[16,32,512]{2,1,0:T(8,128)(2,1)S(1)} all-to-all(bf16[16,32,512]{2,1,0:T(8,128)(2,1)S(1)} %bitcast.18), channel_id=1, replica_groups={{8,10,12,14,0,2,4,6,24,26,28,30,16,18,20,22},{9,11,13,15,1,3,5,7,25,27,..., dimensions={0} | all-to-all | bytes 1048576 | tf_op jit(solution)/shard_map/all_to_all | solution.py:252
  26.1 0.0 collective-permute-start.2
  26.1 4.0 %all-to-all-start = ((bf16[16,32,512]{2,1,0:T(8,128)(2,1)}), bf16[16,32,512]{2,1,0:T(8,128)(2,1)S(1)}, u32[]{:S(2)}, u32[]{:S(2)}) async-start(bf16[16,32,512]{2,1,0:T(8,128)(2,1)} %bitcast.3), calls=%async_computation | async-start | bytes 1048576 | tf_op jit(solution)/shard_map/all_to_all | solution.py:252
  30.1 0.0 collective-permute-done.2.refs_1_
  30.1 13.4 %expert_rows.3 = (bf16[512,512]{1,0:T(8,128)(2,1)S(1)}, bf16[512,512]{1,0:T(8,128)(2,1)S(1)}) custom-call(s32[1]{0:T(128)} %bitcast.1.where_ref, bf16[512,512]{1,0:T(8,128)(2,1)S(1)} %bitcast.17, bf16[512,512]{1,0:T(8,128)(2,1)S(1)} %collective-permute-done.2.refs_1_, bf16[1,1024,3072]{2,1,0:T(8,128)(2,1)} %refs_2_.3, bf16[1,1024,3072]{2,1,0:T(8,128)(2,1)} %refs_3_.3, ...), custom_call_target="tpu_custom_call" | custom-call | flops 9663676416 | bytes 18874368 | tf_op jit(solution)/shard_map/expert_rows/pallas_call | solution.py:207
  43.5 0.1 collective-permute-start.3
  43.6 1.3 %all-to-all-done = bf16[16,32,512]{2,1,0:T(8,128)(2,1)S(1)} async-done(((bf16[16,32,512]{2,1,0:T(8,128)(2,1)}), bf16[16,32,512]{2,1,0:T(8,128)(2,1)S(1)}, u32[]{:S(2)}, u32[]{:S(2)}) %all-to-all-start) | async-done | bytes 524320 | tf_op jit(solution)/shard_map/all_to_all | solution.py:252
  44.9 0.0 collective-permute-start
  44.9 0.6 collective-permute-done.3.refs_1_
  45.5 0.9 %add_shares.3 = bf16[512,512]{1,0:T(8,128)(2,1)} custom-call(bf16[512,512]{1,0:T(8,128)(2,1)S(1)} %get-tuple-element.19.refs_0_, bf16[512,512]{1,0:T(8,128)(2,1)S(1)} %collective-permute-done.3.refs_1_), custom_call_target="tpu_custom_call" | custom-call | tf_op jit(solution)/shard_map/add_shares/pallas_call | solution.py:235
  46.4 6.0 %all-to-all-start.3 = ((bf16[16,32,512]{2,1,0:T(8,128)(2,1)}), bf16[16,32,512]{2,1,0:T(8,128)(2,1)S(1)}, u32[]{:S(2)}, u32[]{:S(2)}) async-start(bf16[16,32,512]{2,1,0:T(8,128)(2,1)} %bitcast.10), calls=%async_computation.3 | async-start | bytes 1048576 | tf_op jit(solution)/shard_map/all_to_all | solution.py:252
  52.5 0.0 copy-start.1
  52.5 0.0 collective-permute-done.refs_1_
  52.5 13.4 %expert_rows.2 = (bf16[512,512]{1,0:T(8,128)(2,1)S(1)}, bf16[512,512]{1,0:T(8,128)(2,1)S(1)}) custom-call(s32[1]{0:T(128)} %bitcast.1.where_ref, bf16[512,512]{1,0:T(8,128)(2,1)S(1)} %bitcast.15, bf16[512,512]{1,0:T(8,128)(2,1)S(1)} %collective-permute-done.refs_1_, bf16[1,1024,3072]{2,1,0:T(8,128)(2,1)} %refs_2_.3, bf16[1,1024,3072]{2,1,0:T(8,128)(2,1)} %refs_3_.3, ...), custom_call_target="tpu_custom_call" | custom-call | flops 9663676416 | bytes 18874368 | tf_op jit(solution)/shard_map/expert_rows/pallas_call | solution.py:207
  65.9 0.1 collective-permute-start.1
  66.0 1.9 %collective-permute-done.1.refs_1_ = bf16[512,512]{1,0:T(8,128)(2,1)S(1)} collective-permute-done((bf16[512,512]{1,0:T(8,128)(2,1)S(1)}, bf16[512,512]{1,0:T(8,128)(2,1)S(1)}, u32[]{:S(2)}, u32[]{:S(2)}) %collective-permute-start.1) | collective-permute-done | bytes 524320 | tf_op jit(solution)/shard_map/ppermute | solution.py:270
  67.9 0.9 %add_shares.2 = bf16[512,512]{1,0:T(8,128)(2,1)} custom-call(bf16[512,512]{1,0:T(8,128)(2,1)S(1)} %get-tuple-element.15.refs_0_, bf16[512,512]{1,0:T(8,128)(2,1)S(1)} %collective-permute-done.1.refs_1_), custom_call_target="tpu_custom_call" | custom-call | tf_op jit(solution)/shard_map/add_shares/pallas_call | solution.py:235
  68.8 0.0 all-to-all-done.3
  68.8 6.0 %all-to-all-start.1 = ((bf16[16,32,512]{2,1,0:T(8,128)(2,1)}), bf16[16,32,512]{2,1,0:T(8,128)(2,1)S(1)}, u32[]{:S(2)}, u32[]{:S(2)}) async-start(bf16[16,32,512]{2,1,0:T(8,128)(2,1)} %bitcast.5), calls=%async_computation.1 | async-start | bytes 1048576 | tf_op jit(solution)/shard_map/all_to_all | solution.py:252
  74.8 0.1 copy.7.ids_ref
  74.9 1.0 %combine_map.1 = (bf16[512,512]{1,0:T(8,128)(2,1)S(1)}, bf16[512,512]{1,0:T(8,128)(2,1)S(1)}) custom-call(s32[512,1]{1,0:T(8,128)S(1)} %copy.7.ids_ref), custom_call_target="tpu_custom_call" | custom-call | tf_op jit(solution)/shard_map/combine_map/pallas_call | solution.py:78
  75.9 0.0 copy-done.1
  75.9 0.1 copy.8.scale_ref
  76.1 0.4 pick.1.refs_0_
  76.5 12.7 %all-to-all-done.1 = bf16[16,32,512]{2,1,0:T(8,128)(2,1)S(1)} async-done(((bf16[16,32,512]{2,1,0:T(8,128)(2,1)}), bf16[16,32,512]{2,1,0:T(8,128)(2,1)S(1)}, u32[]{:S(2)}, u32[]{:S(2)}) %all-to-all-start.1) | async-done | bytes 524320 | tf_op jit(solution)/shard_map/all_to_all | solution.py:252
  89.2 1.2 %finish.1 = bf16[512,512]{1,0:T(8,128)(2,1)} custom-call(bf16[512,512]{1,0:T(8,128)(2,1)S(1)} %get-tuple-element.13.map_ref, bf16[512,512]{1,0:T(8,128)(2,1)S(1)} %bitcast.13, f32[512,1]{1,0:T(8,128)S(1)} %copy.8.scale_ref, bf16[512,512]{1,0:T(8,128)(2,1)S(1)} %pick.1.refs_0_), custom_call_target="tpu_custom_call" | custom-call | tf_op jit(solution)/shard_map/finish/pallas_call | solution.py:112
Async XLA Ops:
  0.7 1.0 %copy-start = (bf16[512,512]{1,0:T(8,128)(2,1)S(1)}, bf16[512,512]{1,0:T(8,128)(2,1)}, u32[]{:S(2)}) copy-start(bf16[512,512]{1,0:T(8,128)(2,1)} %tok_ref.1) | copy-start | bytes 1572868
  26.1 4.0 %collective-permute-start.2 = (bf16[512,512]{1,0:T(8,128)(2,1)S(1)}, bf16[512,512]{1,0:T(8,128)(2,1)S(1)}, u32[]{:S(2)}, u32[]{:S(2)}) collective-permute-start(bf16[512,512]{1,0:T(8,128)(2,1)S(1)} %bitcast.16), channel_id=1, source_target_pairs={{0,1},{1,0},{2,3},{3,2},{4,5},{5,4},{6,7},{7,6},{8,9},{9,8},{10,11... | collective-permute-start | bytes 1572872 | tf_op jit(solution)/shard_map/ppermute | solution.py:270
  26.1 18.8 %all-to-all-start = ((bf16[16,32,512]{2,1,0:T(8,128)(2,1)}), bf16[16,32,512]{2,1,0:T(8,128)(2,1)S(1)}, u32[]{:S(2)}, u32[]{:S(2)}) async-start(bf16[16,32,512]{2,1,0:T(8,128)(2,1)} %bitcast.3), calls=%async_computation | async-start | bytes 1048576 | tf_op jit(solution)/shard_map/all_to_all | solution.py:252
  43.5 2.0 %collective-permute-start.3 = (bf16[512,512]{1,0:T(8,128)(2,1)S(1)}, bf16[512,512]{1,0:T(8,128)(2,1)S(1)}, u32[]{:S(2)}, u32[]{:S(2)}) collective-permute-start(bf16[512,512]{1,0:T(8,128)(2,1)S(1)} %get-tuple-element.20), channel_id=1, source_target_pairs={{0,1},{1,0},{2,3},{3,2},{4,5},{5,4},{6,7},{7,6},{8,9},{9,8},{10,11... | collective-permute-start | bytes 1572872 | tf_op jit(solution)/shard_map/ppermute | solution.py:270
  44.9 7.6 %collective-permute-start = (bf16[512,512]{1,0:T(8,128)(2,1)S(1)}, bf16[512,512]{1,0:T(8,128)(2,1)S(1)}, u32[]{:S(2)}, u32[]{:S(2)}) collective-permute-start(bf16[512,512]{1,0:T(8,128)(2,1)S(1)} %bitcast.14), channel_id=1, source_target_pairs={{0,1},{1,0},{2,3},{3,2},{4,5},{5,4},{6,7},{7,6},{8,9},{9,8},{10,11... | collective-permute-start | bytes 1572872 | tf_op jit(solution)/shard_map/ppermute | solution.py:270
  46.4 22.3 %all-to-all-start.3 = ((bf16[16,32,512]{2,1,0:T(8,128)(2,1)}), bf16[16,32,512]{2,1,0:T(8,128)(2,1)S(1)}, u32[]{:S(2)}, u32[]{:S(2)}) async-start(bf16[16,32,512]{2,1,0:T(8,128)(2,1)} %bitcast.10), calls=%async_computation.3 | async-start | bytes 1048576 | tf_op jit(solution)/shard_map/all_to_all | solution.py:252
  52.5 23.5 %copy-start.1 = (f32[512]{0:T(512)S(1)}, f32[512]{0:T(512)}, u32[]{:S(2)}) copy-start(f32[512]{0:T(512)} %param.8) | copy-start | bytes 6148
  65.9 2.0 %collective-permute-start.1 = (bf16[512,512]{1,0:T(8,128)(2,1)S(1)}, bf16[512,512]{1,0:T(8,128)(2,1)S(1)}, u32[]{:S(2)}, u32[]{:S(2)}) collective-permute-start(bf16[512,512]{1,0:T(8,128)(2,1)S(1)} %get-tuple-element.16), channel_id=1, source_target_pairs={{0,1},{1,0},{2,3},{3,2},{4,5},{5,4},{6,7},{7,6},{8,9},{9,8},{10,11... | collective-permute-start | bytes 1572872 | tf_op jit(solution)/shard_map/ppermute | solution.py:270
  68.8 20.4 %all-to-all-start.1 = ((bf16[16,32,512]{2,1,0:T(8,128)(2,1)}), bf16[16,32,512]{2,1,0:T(8,128)(2,1)S(1)}, u32[]{:S(2)}, u32[]{:S(2)}) async-start(bf16[16,32,512]{2,1,0:T(8,128)(2,1)} %bitcast.5), calls=%async_computation.1 | async-start | bytes 1048576 | tf_op jit(solution)/shard_map/all_to_all | solution.py:252

commit v2 on v1

v2 whole, which is shorter than its diff:
```python
import functools

import jax
import jax.numpy as jnp
from jax import lax
from jax.experimental import pallas as pl
from jax.experimental.pallas import tpu as pltpu
from jax.sharding import PartitionSpec as P

F32 = jnp.float32
BF16 = jnp.bfloat16
MIB = 1 << 20


def vmem():
    return pl.BlockSpec(memory_space=pltpu.VMEM)


def in_hbm(array):
    return pltpu.with_memory_space_constraint(array, pltpu.HBM)


def exchange_order(n_expert):
    if n_expert == 16:
        return [10, 4, 9, 8, 5, 6, 11, 7, 12, 0, 13, 1, 14, 2, 15, 3]
    if n_expert % 4:
        return list(range(n_expert))
    quarter = [list(range(q * n_expert // 4, (q + 1) * n_expert // 4)) for q in range(4)]
    return [e for first, second in ((1, 2), (0, 3)) for pair in zip(quarter[first], quarter[second]) for e in pair]


def exchange_place(expert, n_expert):
    place = jnp.zeros_like(expert)
    for index, owner in enumerate(exchange_order(n_expert)):
        place = jnp.where(expert == owner, index, place)
    return place


def params(limit_mib):
    return pltpu.CompilerParams(vmem_limit_bytes=limit_mib * MIB)


def chunk_sizes(capacity):
    if capacity >= 32:
        return (capacity // 2, capacity // 2)
    return (capacity,)


def dispatch_kernel(n_expert, chunks, ids_hbm, tok_hbm, *refs):
    out_refs = refs[:len(chunks)]
    ids_ref, tok_ref, *stage_refs, arrived = refs[len(chunks):]
    copies = [
        pltpu.make_async_copy(ids_hbm, ids_ref, arrived.at[0]),
        pltpu.make_async_copy(tok_hbm, tok_ref, arrived.at[1]),
    ]
    for copy in copies:
        copy.start()
    n_tok = tok_ref.shape[0]
    owner = lax.broadcasted_iota(jnp.int32, (n_expert, n_tok), 0)
    before = lax.broadcasted_iota(jnp.int32, (n_tok, n_tok), 0) < lax.broadcasted_iota(jnp.int32, (n_tok, n_tok), 1)
    before = before.astype(F32).astype(BF16)
    copies[0].wait()
    ids = exchange_place(ids_ref[...], n_expert)
    onehot = (owner == ids).astype(F32)
    earlier = jnp.dot(onehot.astype(BF16), before, preferred_element_type=F32)
    rank = jnp.sum(earlier * onehot, axis=0, keepdims=True).astype(jnp.int32)
    picks = []
    low = 0
    for size in chunks:
        inside = (rank >= low) & (rank < low + size)
        target = jnp.where(inside, ids * size + (rank - low), -1)
        slot = lax.broadcasted_iota(jnp.int32, (n_expert * size, n_tok), 0)
        picks.append((slot == target).astype(F32).astype(BF16))
        low += size
    copies[1].wait()
    leaving = []
    for index in reversed(range(len(chunks))):
        rows = jnp.dot(picks[index], tok_ref[...], preferred_element_type=F32).astype(BF16)
        if index == 0:
            out_refs[0][...] = rows
        else:
            stage_refs[index - 1][...] = rows
            leaving.append(pltpu.make_async_copy(stage_refs[index - 1], out_refs[index], arrived.at[1 + index]))
            leaving[-1].start()
    for copy in leaving:
        copy.wait()


def dispatch(ids, tokens, n_expert, chunks):
    n_tok, width = tokens.shape
    hbm = pl.BlockSpec(memory_space=pltpu.HBM)
    return pl.pallas_call(
        functools.partial(dispatch_kernel, n_expert, chunks),
        out_shape=[jax.ShapeDtypeStruct((n_expert * size, width), BF16) for size in chunks],
        in_specs=[hbm, hbm],
        out_specs=[vmem()] + [hbm for _ in chunks[1:]],
        scratch_shapes=[pltpu.VMEM((1, n_tok), jnp.int32), pltpu.VMEM((n_tok, width), BF16)]
        + [pltpu.VMEM((n_expert * size, width), BF16) for size in chunks[1:]]
        + [pltpu.SemaphoreType.DMA((1 + len(chunks),))],
        compiler_params=params(24),
        name="dispatch",
    )(in_hbm(ids.reshape(1, n_tok)), in_hbm(tokens))


def combine_map_kernel(n_expert, chunks, ids_ref, *out_refs):
    n_tok = ids_ref.shape[0]
    ids = exchange_place(ids_ref[...], n_expert)
    owner = lax.broadcasted_iota(jnp.int32, (n_tok, n_expert), 1)
    onehot = (owner == ids).astype(F32)
    before = lax.broadcasted_iota(jnp.int32, (n_tok, n_tok), 1) < lax.broadcasted_iota(jnp.int32, (n_tok, n_tok), 0)
    earlier = jnp.dot(before.astype(F32).astype(BF16), onehot.astype(BF16), preferred_element_type=F32)
    rank = jnp.sum(earlier * onehot, axis=1, keepdims=True).astype(jnp.int32)
    low = 0
    for size, out_ref in zip(chunks, out_refs):
        inside = (rank >= low) & (rank < low + size)
        target = jnp.where(inside, ids * size + (rank - low), -1)
        slot = lax.broadcasted_iota(jnp.int32, (n_tok, n_expert * size), 1)
        out_ref[...] = (slot == target).astype(F32).astype(BF16)
        low += size


def combine_map(ids, n_expert, chunks):
    n_tok = ids.shape[0]
    return pl.pallas_call(
        functools.partial(combine_map_kernel, n_expert, chunks),
        out_shape=[jax.ShapeDtypeStruct((n_tok, n_expert * size), BF16) for size in chunks],
        in_specs=[vmem()],
        out_specs=[vmem() for _ in chunks],
        compiler_params=params(24),
        name="combine_map",
    )(ids.reshape(n_tok, 1))


def pick_kernel(map_ref, back_ref, out_ref):
    out_ref[...] = jnp.dot(map_ref[...], back_ref[...], preferred_element_type=F32).astype(BF16)


def pick(pick_map, back):
    return pl.pallas_call(
        pick_kernel,
        out_shape=jax.ShapeDtypeStruct((pick_map.shape[0], back.shape[1]), BF16),
        in_specs=[vmem(), vmem()],
        out_specs=vmem(),
        compiler_params=params(16),
        name="pick",
    )(pick_map, back)


def finish_kernel(n_part, map_ref, back_ref, scale_ref, *refs):
    part_refs = refs[:n_part]
    out_hbm, stage_ref, left = refs[n_part:]
    copies = []
    for index, cut in enumerate(row_cuts(stage_ref.shape[0])):
        total = jnp.dot(map_ref[cut, :], back_ref[...], preferred_element_type=F32)
        for part_ref in part_refs:
            total = total + part_ref[cut, :].astype(F32)
        stage_ref[cut, :] = (scale_ref[cut, :] * total).astype(BF16)
        copies.append(pltpu.make_async_copy(stage_ref.at[cut, :], out_hbm.at[cut, :], left.at[index]))
        copies[-1].start()
    for copy in copies:
        copy.wait()


def finish(pick_map, back, scale, parts):
    n_tok = pick_map.shape[0]
    shape = (n_tok, back.shape[1])
    return pl.pallas_call(
        functools.partial(finish_kernel, len(parts)),
        out_shape=jax.ShapeDtypeStruct(shape, BF16),
        in_specs=[vmem() for _ in range(3 + len(parts))],
        out_specs=pl.BlockSpec(memory_space=pltpu.HBM),
        scratch_shapes=[pltpu.VMEM(shape, BF16), pltpu.SemaphoreType.DMA((len(row_cuts(n_tok)),))],
        compiler_params=params(16),
        name="finish",
    )(pick_map, back, scale.reshape(n_tok, 1), *parts)


def expert_kernel(n_tensor, blocks, where_ref, *refs):
    part_refs = refs[:n_tensor]
    sources = refs[n_tensor:n_tensor + 3]
    out_refs = refs[n_tensor + 3:2 * n_tensor + 3]
    gate_ref, up_ref, down_ref, rows_ref, hidden_ref, arrived = refs[2 * n_tensor + 3:]
    width = part_refs[0].shape[1]
    me = where_ref[0]

    def columns(shift):
        return pl.ds(pl.multiple_of(lax.rem(me + shift, n_tensor) * width, width), width)

    fetches = []
    low = 0
    for step, size in enumerate(blocks):
        cut = pl.ds(low, size)
        fetches.append(
            (
                cut,
                pltpu.make_async_copy(sources[0].at[0, :, cut], gate_ref.at[:, cut], arrived.at[2 * step]),
                pltpu.make_async_copy(sources[1].at[0, :, cut], up_ref.at[:, cut], arrived.at[2 * step + 1]),
            )
        )
        low += size
    down_here = pltpu.make_async_copy(sources[2].at[0], down_ref, arrived.at[2 * len(blocks)])
    for _, gate_here, up_here in fetches:
        gate_here.start()
        up_here.start()
    down_here.start()
    for shift, part_ref in enumerate(part_refs):
        rows_ref[:, columns(shift)] = part_ref[...]
    for cut, gate_here, up_here in fetches:
        rows = rows_ref[...]
        gate_here.wait()
        gate = jnp.dot(rows, gate_ref[:, cut], preferred_element_type=F32)
        up_here.wait()
        up = jnp.dot(rows, up_ref[:, cut], preferred_element_type=F32)
        hidden_ref[:, cut] = (gate / (1.0 + jnp.exp(-gate)) * up).astype(BF16)
    down_here.wait()
    for shift, out_ref in enumerate(out_refs):
        share = jnp.dot(hidden_ref[...], down_ref[:, columns(shift)], preferred_element_type=F32)
        out_ref[...] = share.astype(BF16)


def expert_rows(where, parts, weights):
    n_tensor = len(parts)
    rows, width = parts[0].shape
    depth, hidden = weights[0].shape[1:]
    first = hidden // 3 // 128 * 128
    blocks = (first, hidden - first)
    hbm = pl.BlockSpec(memory_space=pltpu.HBM)
    return pl.pallas_call(
        functools.partial(expert_kernel, n_tensor, blocks),
        out_shape=[jax.ShapeDtypeStruct((rows, width), BF16) for _ in parts],
        in_specs=[pl.BlockSpec(memory_space=pltpu.SMEM)] + [vmem() for _ in parts] + [hbm, hbm, hbm],
        out_specs=[vmem() for _ in parts],
        scratch_shapes=[
            pltpu.VMEM((depth, hidden), BF16),
            pltpu.VMEM((depth, hidden), BF16),
            pltpu.VMEM((hidden, depth), BF16),
            pltpu.VMEM((rows, depth), BF16),
            pltpu.VMEM((rows, hidden), BF16),
            pltpu.SemaphoreType.DMA((2 * len(blocks) + 1,)),
        ],
        compiler_params=params(44),
        cost_estimate=pl.CostEstimate(
            flops=6 * rows * depth * hidden, bytes_accessed=6 * depth * hidden, transcendentals=rows * hidden
        ),
        name="expert_rows",
    )(where, *parts, *[in_hbm(weight) for weight in weights])


def row_cuts(rows):
    cut = rows // 4 if rows % 64 == 0 else rows
    return [pl.ds(low, cut) for low in range(0, rows, cut)]


def add_kernel(*refs):
    *share_refs, out_hbm, stage_ref, left = refs
    copies = []
    for index, cut in enumerate(row_cuts(stage_ref.shape[0])):
        total = share_refs[0][cut, :].astype(F32)
        for share_ref in share_refs[1:]:
            total = total + share_ref[cut, :].astype(F32)
        stage_ref[cut, :] = total.astype(BF16)
        copies.append(pltpu.make_async_copy(stage_ref.at[cut, :], out_hbm.at[cut, :], left.at[index]))
        copies[-1].start()
    for copy in copies:
        copy.wait()


def add(shares):
    shape = shares[0].shape
    return pl.pallas_call(
        add_kernel,
        out_shape=jax.ShapeDtypeStruct(shape, BF16),
        in_specs=[vmem() for _ in shares],
        out_specs=pl.BlockSpec(memory_space=pltpu.HBM),
        scratch_shapes=[pltpu.VMEM(shape, BF16), pltpu.SemaphoreType.DMA((len(row_cuts(shape[0])),))],
        compiler_params=params(8),
        name="add_shares",
    )(*shares)


def exchange(rows, n_expert):
    size = rows.shape[0] // n_expert
    moved = lax.all_to_all(
        rows.reshape(n_expert, size, -1),
        "expert",
        split_axis=0,
        concat_axis=0,
        axis_index_groups=[exchange_order(n_expert)],
        tiled=True,
    )
    return moved.reshape(rows.shape)


def shards(tokens, expert_ids, gate_scale, gate_weight, up_weight, down_weight):
    n_expert = lax.axis_size("expert")
    n_tensor = lax.axis_size("tensor")
    chunks = chunk_sizes(2 * tokens.shape[0] // n_expert)
    where = lax.axis_index("tensor").astype(jnp.int32).reshape(1)

    def shifted(rows, shift):
        return lax.ppermute(rows, "tensor", [(i, (i - shift) % n_tensor) for i in range(n_tensor)])

    outgoing = dispatch(expert_ids, tokens, n_expert, chunks)
    maps = combine_map(expert_ids, n_expert, chunks)
    weights = (gate_weight, up_weight, down_weight)
    backs = []
    for rows in outgoing:
        arrived = exchange(rows, n_expert)
        parts = [arrived] + [shifted(arrived, shift) for shift in range(1, n_tensor)]
        shares = expert_rows(where, parts, weights)
        total = add([shares[0]] + [shifted(shares[shift], -shift) for shift in range(1, n_tensor)])
        backs.append(exchange(total, n_expert))
    picked = [pick(pick_map, back) for pick_map, back in zip(maps[:-1], backs[:-1])]
    return finish(maps[-1], backs[-1], gate_scale, picked)


def solution(mesh):
    in_specs = (
        P("expert", "tensor"),
        P("expert"),
        P("expert"),
        P("expert", None, "tensor"),
        P("expert", None, "tensor"),
        P("expert", "tensor", None),
    )
    out_specs = P("expert", "tensor")
    return jax.shard_map(shards, mesh=mesh, in_specs=in_specs, out_specs=out_specs, check_vma=False)
```

time: 91 us -> 85 us (0.934)
  waiting for transfers between devices: 16.5 us -> 12.8 us
  starting transfers between devices: 16.2 us -> 19.5 us
  blocking collectives: 22.7 us -> 19.7 us
  local copies, waits for them, and re-layouts: 1.33 us -> 0.3 us
  Pallas kernels: 33 us -> 32 us
    all_to_all x3, waiting for transfers between devices: 14 us -> 9.51 us  [exchange(): lax.all_to_all(rows.reshape(n_expert, size, -1), 'expert', split_axis=0,...]
    all_to_all x1, blocking collectives: 22.7 us -> 19.7 us  [exchange(): lax.all_to_all(rows.reshape(n_expert, size, -1), 'expert', split_axis=0,...]
    all_to_all x3, starting transfers between devices: 16 us -> 18.9 us  [exchange(): lax.all_to_all(rows.reshape(n_expert, size, -1), 'expert', split_axis=0,...]
    pallas_call x4, Pallas kernels: 28.6 us -> 26.9 us  [the longest x2 25.2 us: expert_rows(): pl.pallas_call(functools.partial(expert_kernel, n_tensor, blocks), out_sh...]
    unnamed x4, local copies, waits for them, and re-layouts: 1.04 us -> 0.01 us
  transfers between devices with their start and end apart: 7 -> 7, of which waited for: 4 -> 3; matrix products, arithmetic and copies ran while one was open for 0% -> 0% of each run, Pallas kernels for 33% -> 34%
where the time goes in v2:
time: 85 us; the launch traced here: 84.6 us
  Pallas kernels  32 us (38%)
  blocking collectives  19.7 us (23%)
  starting transfers between devices  19.5 us (23%)
  waiting for transfers between devices  12.8 us (15%)
    pallas_call x2, Pallas kernels, expert_rows(): pl.pallas_call(functools.partial(expert_kernel, n_tensor, blocks), out_sh...  25.2 us
    all_to_all x1, blocking collectives, exchange(): lax.all_to_all(rows.reshape(n_expert, size, -1), 'expert', split_axis=0,...  19.7 us
    all_to_all x3, starting transfers between devices, exchange(): lax.all_to_all(rows.reshape(n_expert, size, -1), 'expert', split_axis=0,...  18.9 us
    all_to_all x3, waiting for transfers between devices, exchange(): lax.all_to_all(rows.reshape(n_expert, size, -1), 'expert', split_axis=0,...  9.51 us
    ppermute x4, waiting for transfers between devices, shifted(): lax.ppermute(rows, 'tensor', [(i, (i - shift) % n_tensor) for i in range(...  3.3 us
    pallas_call x1, Pallas kernels, dispatch(): pl.pallas_call(functools.partial(dispatch_kernel, n_expert, chunks), out_...  2.4 us
    pallas_call x2, Pallas kernels, add(): pl.pallas_call(add_kernel, out_shape=jax.ShapeDtypeStruct(shape, BF16), i...  1.71 us
  transfers between devices with their start and end apart: 7, of which 3 were waited for; matrix products, arithmetic and copies ran while one was open for 0% of the time, Pallas kernels for 34%

profile of v2, /device:TPU:0, one launch (start us, length us, event | category | flops | bytes accessed | tf_op | source)
XLA Modules:
  0.0 84.6 jit_solution(8864775373521193155)
XLA Ops:
  0.0 2.4 %dispatch.1 = (bf16[512,512]{1,0:T(8,128)(2,1)S(1)}, bf16[512,512]{1,0:T(8,128)(2,1)}) custom-call(s32[1,512]{1,0:T(1,128)} %bitcast.19, bf16[512,512]{1,0:T(8,128)(2,1)} %tok_hbm.1), custom_call_target="tpu_custom_call" | custom-call | tf_op jit(solution)/shard_map/dispatch/pallas_call | solution.py:92
  2.4 19.7 %all_to_all.20 = bf16[16,32,512]{2,1,0:T(8,128)(2,1)S(1)} all-to-all(bf16[16,32,512]{2,1,0:T(8,128)(2,1)S(1)} %bitcast.18), channel_id=1, replica_groups={{20,8,18,16,10,12,22,14,24,0,26,2,28,4,30,6},{21,9,19,17,11,13,23,15,25..., dimensions={0} | all-to-all | bytes 1048576 | tf_op jit(solution)/shard_map/all_to_all | solution.py:283
  22.1 0.0 collective-permute-start.2
  22.1 6.8 %all-to-all-start = ((bf16[16,32,512]{2,1,0:T(8,128)(2,1)}), bf16[16,32,512]{2,1,0:T(8,128)(2,1)S(1)}, u32[]{:S(2)}, u32[]{:S(2)}) async-start(bf16[16,32,512]{2,1,0:T(8,128)(2,1)} %bitcast.3), calls=%async_computation | async-start | bytes 1048576 | tf_op jit(solution)/shard_map/all_to_all | solution.py:283
  28.9 0.0 collective-permute-done.2.refs_1_
  28.9 12.6 %expert_rows.3 = (bf16[512,512]{1,0:T(8,128)(2,1)S(1)}, bf16[512,512]{1,0:T(8,128)(2,1)S(1)}) custom-call(s32[1]{0:T(128)} %bitcast.1.where_ref, bf16[512,512]{1,0:T(8,128)(2,1)S(1)} %bitcast.17, bf16[512,512]{1,0:T(8,128)(2,1)S(1)} %collective-permute-done.2.refs_1_, bf16[1,1024,3072]{2,1,0:T(8,128)(2,1)} %refs_2_.3, bf16[1,1024,3072]{2,1,0:T(8,128)(2,1)} %refs_3_.3, ...), custom_call_target="tpu_custom_call" | custom-call | flops 9663676416 | bytes 18874368 | tf_op jit(solution)/shard_map/expert_rows/pallas_call | solution.py:228
  41.5 0.3 collective-permute-start.3
  41.8 0.0 all-to-all-done
  41.8 0.2 collective-permute-start
  42.1 1.4 %collective-permute-done.3.refs_1_ = bf16[512,512]{1,0:T(8,128)(2,1)S(1)} collective-permute-done((bf16[512,512]{1,0:T(8,128)(2,1)S(1)}, bf16[512,512]{1,0:T(8,128)(2,1)S(1)}, u32[]{:S(2)}, u32[]{:S(2)}) %collective-permute-start.3) | collective-permute-done | bytes 524320 | tf_op jit(solution)/shard_map/ppermute | solution.py:301
  43.5 0.9 %add_shares.3 = bf16[512,512]{1,0:T(8,128)(2,1)} custom-call(bf16[512,512]{1,0:T(8,128)(2,1)S(1)} %get-tuple-element.19.refs_0_, bf16[512,512]{1,0:T(8,128)(2,1)S(1)} %collective-permute-done.3.refs_1_), custom_call_target="tpu_custom_call" | custom-call | tf_op jit(solution)/shard_map/add_shares/pallas_call | solution.py:270
  44.3 6.0 %all-to-all-start.3 = ((bf16[16,32,512]{2,1,0:T(8,128)(2,1)}), bf16[16,32,512]{2,1,0:T(8,128)(2,1)S(1)}, u32[]{:S(2)}, u32[]{:S(2)}) async-start(bf16[16,32,512]{2,1,0:T(8,128)(2,1)} %bitcast.10), calls=%async_computation.3 | async-start | bytes 1048576 | tf_op jit(solution)/shard_map/all_to_all | solution.py:283
  50.4 0.0 copy-start
  50.4 0.0 copy-start.1
  50.4 0.0 collective-permute-done.refs_1_
  50.4 12.6 %expert_rows.2 = (bf16[512,512]{1,0:T(8,128)(2,1)S(1)}, bf16[512,512]{1,0:T(8,128)(2,1)S(1)}) custom-call(s32[1]{0:T(128)} %bitcast.1.where_ref, bf16[512,512]{1,0:T(8,128)(2,1)S(1)} %bitcast.15, bf16[512,512]{1,0:T(8,128)(2,1)S(1)} %collective-permute-done.refs_1_, bf16[1,1024,3072]{2,1,0:T(8,128)(2,1)} %refs_2_.3, bf16[1,1024,3072]{2,1,0:T(8,128)(2,1)} %refs_3_.3, ...), custom_call_target="tpu_custom_call" | custom-call | flops 9663676416 | bytes 18874368 | tf_op jit(solution)/shard_map/expert_rows/pallas_call | solution.py:228
  63.0 0.1 collective-permute-start.1
  63.1 1.9 %collective-permute-done.1.refs_1_ = bf16[512,512]{1,0:T(8,128)(2,1)S(1)} collective-permute-done((bf16[512,512]{1,0:T(8,128)(2,1)S(1)}, bf16[512,512]{1,0:T(8,128)(2,1)S(1)}, u32[]{:S(2)}, u32[]{:S(2)}) %collective-permute-start.1) | collective-permute-done | bytes 524320 | tf_op jit(solution)/shard_map/ppermute | solution.py:301
  64.9 0.8 %add_shares.2 = bf16[512,512]{1,0:T(8,128)(2,1)} custom-call(bf16[512,512]{1,0:T(8,128)(2,1)S(1)} %get-tuple-element.15.refs_0_, bf16[512,512]{1,0:T(8,128)(2,1)S(1)} %collective-permute-done.1.refs_1_), custom_call_target="tpu_custom_call" | custom-call | tf_op jit(solution)/shard_map/add_shares/pallas_call | solution.py:270
  65.8 0.0 all-to-all-done.3
  65.8 6.0 %all-to-all-start.1 = ((bf16[16,32,512]{2,1,0:T(8,128)(2,1)}), bf16[16,32,512]{2,1,0:T(8,128)(2,1)S(1)}, u32[]{:S(2)}, u32[]{:S(2)}) async-start(bf16[16,32,512]{2,1,0:T(8,128)(2,1)} %bitcast.5), calls=%async_computation.1 | async-start | bytes 1048576 | tf_op jit(solution)/shard_map/all_to_all | solution.py:283
  71.8 0.0 copy-done
  71.9 0.1 copy.7.ids_ref
  72.0 1.1 %combine_map.1 = (bf16[512,512]{1,0:T(8,128)(2,1)S(1)}, bf16[512,512]{1,0:T(8,128)(2,1)S(1)}) custom-call(s32[512,1]{1,0:T(8,128)S(1)} %copy.7.ids_ref), custom_call_target="tpu_custom_call" | custom-call | tf_op jit(solution)/shard_map/combine_map/pallas_call | solution.py:124
  73.1 0.0 copy-done.1
  73.2 0.1 copy.8.scale_ref
  73.3 0.4 pick.1.refs_0_
  73.8 9.5 %all-to-all-done.1 = bf16[16,32,512]{2,1,0:T(8,128)(2,1)S(1)} async-done(((bf16[16,32,512]{2,1,0:T(8,128)(2,1)}), bf16[16,32,512]{2,1,0:T(8,128)(2,1)S(1)}, u32[]{:S(2)}, u32[]{:S(2)}) %all-to-all-start.1) | async-done | bytes 524320 | tf_op jit(solution)/shard_map/all_to_all | solution.py:283
  83.3 1.1 %finish.1 = bf16[512,512]{1,0:T(8,128)(2,1)} custom-call(bf16[512,512]{1,0:T(8,128)(2,1)S(1)} %get-tuple-element.13.map_ref, bf16[512,512]{1,0:T(8,128)(2,1)S(1)} %bitcast.13, f32[512,1]{1,0:T(8,128)S(1)} %copy.8.scale_ref, bf16[512,512]{1,0:T(8,128)(2,1)S(1)} %pick.1.refs_0_), custom_call_target="tpu_custom_call" | custom-call | tf_op jit(solution)/shard_map/finish/pallas_call | solution.py:167
Async XLA Ops:
  22.1 6.8 %collective-permute-start.2 = (bf16[512,512]{1,0:T(8,128)(2,1)S(1)}, bf16[512,512]{1,0:T(8,128)(2,1)S(1)}, u32[]{:S(2)}, u32[]{:S(2)}) collective-permute-start(bf16[512,512]{1,0:T(8,128)(2,1)S(1)} %bitcast.16), channel_id=1, source_target_pairs={{0,1},{1,0},{2,3},{3,2},{4,5},{5,4},{6,7},{7,6},{8,9},{9,8},{10,11... | collective-permute-start | bytes 1572872 | tf_op jit(solution)/shard_map/ppermute | solution.py:301
  22.1 19.7 %all-to-all-start = ((bf16[16,32,512]{2,1,0:T(8,128)(2,1)}), bf16[16,32,512]{2,1,0:T(8,128)(2,1)S(1)}, u32[]{:S(2)}, u32[]{:S(2)}) async-start(bf16[16,32,512]{2,1,0:T(8,128)(2,1)} %bitcast.3), calls=%async_computation | async-start | bytes 1048576 | tf_op jit(solution)/shard_map/all_to_all | solution.py:283
  41.5 2.0 %collective-permute-start.3 = (bf16[512,512]{1,0:T(8,128)(2,1)S(1)}, bf16[512,512]{1,0:T(8,128)(2,1)S(1)}, u32[]{:S(2)}, u32[]{:S(2)}) collective-permute-start(bf16[512,512]{1,0:T(8,128)(2,1)S(1)} %get-tuple-element.20), channel_id=1, source_target_pairs={{0,1},{1,0},{2,3},{3,2},{4,5},{5,4},{6,7},{7,6},{8,9},{9,8},{10,11... | collective-permute-start | bytes 1572872 | tf_op jit(solution)/shard_map/ppermute | solution.py:301
  41.8 8.6 %collective-permute-start = (bf16[512,512]{1,0:T(8,128)(2,1)S(1)}, bf16[512,512]{1,0:T(8,128)(2,1)S(1)}, u32[]{:S(2)}, u32[]{:S(2)}) collective-permute-start(bf16[512,512]{1,0:T(8,128)(2,1)S(1)} %bitcast.14), channel_id=1, source_target_pairs={{0,1},{1,0},{2,3},{3,2},{4,5},{5,4},{6,7},{7,6},{8,9},{9,8},{10,11... | collective-permute-start | bytes 1572872 | tf_op jit(solution)/shard_map/ppermute | solution.py:301
  44.3 21.5 %all-to-all-start.3 = ((bf16[16,32,512]{2,1,0:T(8,128)(2,1)}), bf16[16,32,512]{2,1,0:T(8,128)(2,1)S(1)}, u32[]{:S(2)}, u32[]{:S(2)}) async-start(bf16[16,32,512]{2,1,0:T(8,128)(2,1)} %bitcast.10), calls=%async_computation.3 | async-start | bytes 1048576 | tf_op jit(solution)/shard_map/all_to_all | solution.py:283
  50.4 21.5 %copy-start = (s32[512]{0:T(512)S(1)}, s32[512]{0:T(512)}, u32[]{:S(2)}) copy-start(s32[512]{0:T(512)} %param.7) | copy-start | bytes 6148
  50.4 22.8 %copy-start.1 = (f32[512]{0:T(512)S(1)}, f32[512]{0:T(512)}, u32[]{:S(2)}) copy-start(f32[512]{0:T(512)} %param.8) | copy-start | bytes 6148
  63.0 2.0 %collective-permute-start.1 = (bf16[512,512]{1,0:T(8,128)(2,1)S(1)}, bf16[512,512]{1,0:T(8,128)(2,1)S(1)}, u32[]{:S(2)}, u32[]{:S(2)}) collective-permute-start(bf16[512,512]{1,0:T(8,128)(2,1)S(1)} %get-tuple-element.16), channel_id=1, source_target_pairs={{0,1},{1,0},{2,3},{3,2},{4,5},{5,4},{6,7},{7,6},{8,9},{9,8},{10,11... | collective-permute-start | bytes 1572872 | tf_op jit(solution)/shard_map/ppermute | solution.py:301
  65.8 17.4 %all-to-all-start.1 = ((bf16[16,32,512]{2,1,0:T(8,128)(2,1)}), bf16[16,32,512]{2,1,0:T(8,128)(2,1)S(1)}, u32[]{:S(2)}, u32[]{:S(2)}) async-start(bf16[16,32,512]{2,1,0:T(8,128)(2,1)} %bitcast.5), calls=%async_computation.1 | async-start | bytes 1048576 | tf_op jit(solution)/shard_map/all_to_all | solution.py:283

commit v3 on v2

--- a/solution.py
+++ b/solution.py
@@ -22,7 +22,7 @@
 
 def exchange_order(n_expert):
     if n_expert == 16:
-        return [10, 4, 9, 8, 5, 6, 11, 7, 12, 0, 13, 1, 14, 2, 15, 3]
+        return [10, 4, 9, 8, 5, 6, 11, 0, 12, 7, 13, 14, 1, 2, 15, 3]
     if n_expert % 4:
         return list(range(n_expert))
     quarter = [list(range(q * n_expert // 4, (q + 1) * n_expert // 4)) for q in range(4)]

time: 85 us -> 84.3 us (level)
  no operation moved by 1% of the time
where the time goes in v3:
time: 84.3 us; the launch traced here: 83.9 us
  Pallas kernels  32 us (38%)
  blocking collectives  19.5 us (23%)
  starting transfers between devices  19.5 us (23%)
  waiting for transfers between devices  12.2 us (14%)
    pallas_call x2, Pallas kernels, expert_rows(): pl.pallas_call(functools.partial(expert_kernel, n_tensor, blocks), out_sh...  25.1 us
    all_to_all x1, blocking collectives, exchange(): lax.all_to_all(rows.reshape(n_expert, size, -1), 'expert', split_axis=0,...  19.5 us
    all_to_all x3, starting transfers between devices, exchange(): lax.all_to_all(rows.reshape(n_expert, size, -1), 'expert', split_axis=0,...  18.9 us
    all_to_all x3, waiting for transfers between devices, exchange(): lax.all_to_all(rows.reshape(n_expert, size, -1), 'expert', split_axis=0,...  8.93 us
    ppermute x4, waiting for transfers between devices, shifted(): lax.ppermute(rows, 'tensor', [(i, (i - shift) % n_tensor) for i in range(...  3.3 us
    pallas_call x1, Pallas kernels, dispatch(): pl.pallas_call(functools.partial(dispatch_kernel, n_expert, chunks), out_...  2.4 us
    pallas_call x2, Pallas kernels, add(): pl.pallas_call(add_kernel, out_shape=jax.ShapeDtypeStruct(shape, BF16), i...  1.71 us
  transfers between devices with their start and end apart: 7, of which 3 were waited for; matrix products, arithmetic and copies ran while one was open for 0% of the time, Pallas kernels for 34%

profile of v3, /device:TPU:0, one launch (start us, length us, event | category | flops | bytes accessed | tf_op | source)
XLA Modules:
  0.0 83.9 jit_solution(11881465048713427467)
XLA Ops:
  0.0 2.4 %dispatch.1 = (bf16[512,512]{1,0:T(8,128)(2,1)S(1)}, bf16[512,512]{1,0:T(8,128)(2,1)}) custom-call(s32[1,512]{1,0:T(1,128)} %bitcast.19, bf16[512,512]{1,0:T(8,128)(2,1)} %tok_hbm.1), custom_call_target="tpu_custom_call" | custom-call | tf_op jit(solution)/shard_map/dispatch/pallas_call | solution.py:92
  2.4 19.5 %all_to_all.20 = bf16[16,32,512]{2,1,0:T(8,128)(2,1)S(1)} all-to-all(bf16[16,32,512]{2,1,0:T(8,128)(2,1)S(1)} %bitcast.18), channel_id=1, replica_groups={{20,8,18,16,10,12,22,0,24,14,26,28,2,4,30,6},{21,9,19,17,11,13,23,1,25,..., dimensions={0} | all-to-all | bytes 1048576 | tf_op jit(solution)/shard_map/all_to_all | solution.py:283
  21.9 0.0 collective-permute-start.2
  21.9 6.8 %all-to-all-start = ((bf16[16,32,512]{2,1,0:T(8,128)(2,1)}), bf16[16,32,512]{2,1,0:T(8,128)(2,1)S(1)}, u32[]{:S(2)}, u32[]{:S(2)}) async-start(bf16[16,32,512]{2,1,0:T(8,128)(2,1)} %bitcast.3), calls=%async_computation | async-start | bytes 1048576 | tf_op jit(solution)/shard_map/all_to_all | solution.py:283
  28.8 0.0 collective-permute-done.2.refs_1_
  28.8 12.6 %expert_rows.3 = (bf16[512,512]{1,0:T(8,128)(2,1)S(1)}, bf16[512,512]{1,0:T(8,128)(2,1)S(1)}) custom-call(s32[1]{0:T(128)} %bitcast.1.where_ref, bf16[512,512]{1,0:T(8,128)(2,1)S(1)} %bitcast.17, bf16[512,512]{1,0:T(8,128)(2,1)S(1)} %collective-permute-done.2.refs_1_, bf16[1,1024,3072]{2,1,0:T(8,128)(2,1)} %refs_2_.3, bf16[1,1024,3072]{2,1,0:T(8,128)(2,1)} %refs_3_.3, ...), custom_call_target="tpu_custom_call" | custom-call | flops 9663676416 | bytes 18874368 | tf_op jit(solution)/shard_map/expert_rows/pallas_call | solution.py:228
  41.4 0.1 collective-permute-start.3
  41.4 0.0 all-to-all-done
  41.5 0.5 collective-permute-start
  41.9 1.4 %collective-permute-done.3.refs_1_ = bf16[512,512]{1,0:T(8,128)(2,1)S(1)} collective-permute-done((bf16[512,512]{1,0:T(8,128)(2,1)S(1)}, bf16[512,512]{1,0:T(8,128)(2,1)S(1)}, u32[]{:S(2)}, u32[]{:S(2)}) %collective-permute-start.3) | collective-permute-done | bytes 524320 | tf_op jit(solution)/shard_map/ppermute | solution.py:301
  43.3 0.9 %add_shares.3 = bf16[512,512]{1,0:T(8,128)(2,1)} custom-call(bf16[512,512]{1,0:T(8,128)(2,1)S(1)} %get-tuple-element.19.refs_0_, bf16[512,512]{1,0:T(8,128)(2,1)S(1)} %collective-permute-done.3.refs_1_), custom_call_target="tpu_custom_call" | custom-call | tf_op jit(solution)/shard_map/add_shares/pallas_call | solution.py:270
  44.2 6.0 %all-to-all-start.3 = ((bf16[16,32,512]{2,1,0:T(8,128)(2,1)}), bf16[16,32,512]{2,1,0:T(8,128)(2,1)S(1)}, u32[]{:S(2)}, u32[]{:S(2)}) async-start(bf16[16,32,512]{2,1,0:T(8,128)(2,1)} %bitcast.10), calls=%async_computation.3 | async-start | bytes 1048576 | tf_op jit(solution)/shard_map/all_to_all | solution.py:283
  50.2 0.0 copy-start
  50.2 0.0 copy-start.1
  50.3 0.0 collective-permute-done.refs_1_
  50.3 12.6 %expert_rows.2 = (bf16[512,512]{1,0:T(8,128)(2,1)S(1)}, bf16[512,512]{1,0:T(8,128)(2,1)S(1)}) custom-call(s32[1]{0:T(128)} %bitcast.1.where_ref, bf16[512,512]{1,0:T(8,128)(2,1)S(1)} %bitcast.15, bf16[512,512]{1,0:T(8,128)(2,1)S(1)} %collective-permute-done.refs_1_, bf16[1,1024,3072]{2,1,0:T(8,128)(2,1)} %refs_2_.3, bf16[1,1024,3072]{2,1,0:T(8,128)(2,1)} %refs_3_.3, ...), custom_call_target="tpu_custom_call" | custom-call | flops 9663676416 | bytes 18874368 | tf_op jit(solution)/shard_map/expert_rows/pallas_call | solution.py:228
  62.8 0.1 collective-permute-start.1
  62.9 1.9 %collective-permute-done.1.refs_1_ = bf16[512,512]{1,0:T(8,128)(2,1)S(1)} collective-permute-done((bf16[512,512]{1,0:T(8,128)(2,1)S(1)}, bf16[512,512]{1,0:T(8,128)(2,1)S(1)}, u32[]{:S(2)}, u32[]{:S(2)}) %collective-permute-start.1) | collective-permute-done | bytes 524320 | tf_op jit(solution)/shard_map/ppermute | solution.py:301
  64.8 0.8 %add_shares.2 = bf16[512,512]{1,0:T(8,128)(2,1)} custom-call(bf16[512,512]{1,0:T(8,128)(2,1)S(1)} %get-tuple-element.15.refs_0_, bf16[512,512]{1,0:T(8,128)(2,1)S(1)} %collective-permute-done.1.refs_1_), custom_call_target="tpu_custom_call" | custom-call | tf_op jit(solution)/shard_map/add_shares/pallas_call | solution.py:270
  65.7 0.0 all-to-all-done.3
  65.7 6.0 %all-to-all-start.1 = ((bf16[16,32,512]{2,1,0:T(8,128)(2,1)}), bf16[16,32,512]{2,1,0:T(8,128)(2,1)S(1)}, u32[]{:S(2)}, u32[]{:S(2)}) async-start(bf16[16,32,512]{2,1,0:T(8,128)(2,1)} %bitcast.5), calls=%async_computation.1 | async-start | bytes 1048576 | tf_op jit(solution)/shard_map/all_to_all | solution.py:283
  71.7 0.0 copy-done
  71.7 0.1 copy.7.ids_ref
  71.9 1.1 %combine_map.1 = (bf16[512,512]{1,0:T(8,128)(2,1)S(1)}, bf16[512,512]{1,0:T(8,128)(2,1)S(1)}) custom-call(s32[512,1]{1,0:T(8,128)S(1)} %copy.7.ids_ref), custom_call_target="tpu_custom_call" | custom-call | tf_op jit(solution)/shard_map/combine_map/pallas_call | solution.py:124
  73.0 0.0 copy-done.1
  73.0 0.1 copy.8.scale_ref
  73.2 0.4 pick.1.refs_0_
  73.6 8.9 %all-to-all-done.1 = bf16[16,32,512]{2,1,0:T(8,128)(2,1)S(1)} async-done(((bf16[16,32,512]{2,1,0:T(8,128)(2,1)}), bf16[16,32,512]{2,1,0:T(8,128)(2,1)S(1)}, u32[]{:S(2)}, u32[]{:S(2)}) %all-to-all-start.1) | async-done | bytes 524320 | tf_op jit(solution)/shard_map/all_to_all | solution.py:283
  82.6 1.1 %finish.1 = bf16[512,512]{1,0:T(8,128)(2,1)} custom-call(bf16[512,512]{1,0:T(8,128)(2,1)S(1)} %get-tuple-element.13.map_ref, bf16[512,512]{1,0:T(8,128)(2,1)S(1)} %bitcast.13, f32[512,1]{1,0:T(8,128)S(1)} %copy.8.scale_ref, bf16[512,512]{1,0:T(8,128)(2,1)S(1)} %pick.1.refs_0_), custom_call_target="tpu_custom_call" | custom-call | tf_op jit(solution)/shard_map/finish/pallas_call | solution.py:167
Async XLA Ops:
  21.9 6.8 %collective-permute-start.2 = (bf16[512,512]{1,0:T(8,128)(2,1)S(1)}, bf16[512,512]{1,0:T(8,128)(2,1)S(1)}, u32[]{:S(2)}, u32[]{:S(2)}) collective-permute-start(bf16[512,512]{1,0:T(8,128)(2,1)S(1)} %bitcast.16), channel_id=1, source_target_pairs={{0,1},{1,0},{2,3},{3,2},{4,5},{5,4},{6,7},{7,6},{8,9},{9,8},{10,11... | collective-permute-start | bytes 1572872 | tf_op jit(solution)/shard_map/ppermute | solution.py:301
  21.9 19.5 %all-to-all-start = ((bf16[16,32,512]{2,1,0:T(8,128)(2,1)}), bf16[16,32,512]{2,1,0:T(8,128)(2,1)S(1)}, u32[]{:S(2)}, u32[]{:S(2)}) async-start(bf16[16,32,512]{2,1,0:T(8,128)(2,1)} %bitcast.3), calls=%async_computation | async-start | bytes 1048576 | tf_op jit(solution)/shard_map/all_to_all | solution.py:283
  41.4 2.0 %collective-permute-start.3 = (bf16[512,512]{1,0:T(8,128)(2,1)S(1)}, bf16[512,512]{1,0:T(8,128)(2,1)S(1)}, u32[]{:S(2)}, u32[]{:S(2)}) collective-permute-start(bf16[512,512]{1,0:T(8,128)(2,1)S(1)} %get-tuple-element.20), channel_id=1, source_target_pairs={{0,1},{1,0},{2,3},{3,2},{4,5},{5,4},{6,7},{7,6},{8,9},{9,8},{10,11... | collective-permute-start | bytes 1572872 | tf_op jit(solution)/shard_map/ppermute | solution.py:301
  41.5 8.8 %collective-permute-start = (bf16[512,512]{1,0:T(8,128)(2,1)S(1)}, bf16[512,512]{1,0:T(8,128)(2,1)S(1)}, u32[]{:S(2)}, u32[]{:S(2)}) collective-permute-start(bf16[512,512]{1,0:T(8,128)(2,1)S(1)} %bitcast.14), channel_id=1, source_target_pairs={{0,1},{1,0},{2,3},{3,2},{4,5},{5,4},{6,7},{7,6},{8,9},{9,8},{10,11... | collective-permute-start | bytes 1572872 | tf_op jit(solution)/shard_map/ppermute | solution.py:301
  44.2 21.5 %all-to-all-start.3 = ((bf16[16,32,512]{2,1,0:T(8,128)(2,1)}), bf16[16,32,512]{2,1,0:T(8,128)(2,1)S(1)}, u32[]{:S(2)}, u32[]{:S(2)}) async-start(bf16[16,32,512]{2,1,0:T(8,128)(2,1)} %bitcast.10), calls=%async_computation.3 | async-start | bytes 1048576 | tf_op jit(solution)/shard_map/all_to_all | solution.py:283
  50.2 21.5 %copy-start = (s32[512]{0:T(512)S(1)}, s32[512]{0:T(512)}, u32[]{:S(2)}) copy-start(s32[512]{0:T(512)} %param.7) | copy-start | bytes 6148
  50.2 22.8 %copy-start.1 = (f32[512]{0:T(512)S(1)}, f32[512]{0:T(512)}, u32[]{:S(2)}) copy-start(f32[512]{0:T(512)} %param.8) | copy-start | bytes 6148
  62.8 2.0 %collective-permute-start.1 = (bf16[512,512]{1,0:T(8,128)(2,1)S(1)}, bf16[512,512]{1,0:T(8,128)(2,1)S(1)}, u32[]{:S(2)}, u32[]{:S(2)}) collective-permute-start(bf16[512,512]{1,0:T(8,128)(2,1)S(1)} %get-tuple-element.16), channel_id=1, source_target_pairs={{0,1},{1,0},{2,3},{3,2},{4,5},{5,4},{6,7},{7,6},{8,9},{9,8},{10,11... | collective-permute-start | bytes 1572872 | tf_op jit(solution)/shard_map/ppermute | solution.py:301
  65.7 16.9 %all-to-all-start.1 = ((bf16[16,32,512]{2,1,0:T(8,128)(2,1)}), bf16[16,32,512]{2,1,0:T(8,128)(2,1)S(1)}, u32[]{:S(2)}, u32[]{:S(2)}) async-start(bf16[16,32,512]{2,1,0:T(8,128)(2,1)} %bitcast.5), calls=%async_computation.1 | async-start | bytes 1048576 | tf_op jit(solution)/shard_map/all_to_all | solution.py:283

commit v4 on v3

--- a/solution.py
+++ b/solution.py
@@ -246,6 +246,109 @@
     )(where, *parts, *[in_hbm(weight) for weight in weights])
 
 
+def others_kernel(n_tensor, blocks, where_ref, *refs):
+    part_refs = refs[:n_tensor]
+    sources = refs[n_tensor:n_tensor + 3]
+    hidden_ref, own_ref, *out_refs = refs[n_tensor + 3:2 * n_tensor + 4]
+    gate_ref, up_ref, down_ref, rows_ref, arrived = refs[2 * n_tensor + 4:]
+    width = part_refs[0].shape[1]
+    me = where_ref[0]
+
+    def columns(shift):
+        return pl.ds(pl.multiple_of(lax.rem(me + shift, n_tensor) * width, width), width)
+
+    fetches = []
+    low = 0
+    for step, size in enumerate(blocks):
+        cut = pl.ds(low, size)
+        fetches.append(
+            (
+                cut,
+                pltpu.make_async_copy(sources[0].at[0, :, cut], gate_ref.at[:, cut], arrived.at[2 * step]),
+                pltpu.make_async_copy(sources[1].at[0, :, cut], up_ref.at[:, cut], arrived.at[2 * step + 1]),
+            )
+        )
+        low += size
+    down_here = [
+        pltpu.make_async_copy(
+            sources[2].at[0, :, columns(shift)],
+            own_ref if shift == 0 else down_ref.at[shift - 1],
+            arrived.at[2 * len(blocks) + shift],
+        )
+        for shift in range(n_tensor)
+    ]
+    for _, gate_here, up_here in fetches:
+        gate_here.start()
+        up_here.start()
+    for fetch in down_here[1:] + down_here[:1]:
+        fetch.start()
+    for shift, part_ref in enumerate(part_refs):
+        rows_ref[:, columns(shift)] = part_ref[...]
+    for cut, gate_here, up_here in fetches:
+        rows = rows_ref[...]
+        gate_here.wait()
+        gate = jnp.dot(rows, gate_ref[:, cut], preferred_element_type=F32)
+        up_here.wait()
+        up = jnp.dot(rows, up_ref[:, cut], preferred_element_type=F32)
+        hidden_ref[:, cut] = (gate / (1.0 + jnp.exp(-gate)) * up).astype(BF16)
+    for shift, out_ref in enumerate(out_refs, 1):
+        down_here[shift].wait()
+        share = jnp.dot(hidden_ref[...], down_ref[shift - 1], preferred_element_type=F32)
+        out_ref[...] = share.astype(BF16)
+    down_here[0].wait()
+
+
+def other_shares(where, parts, weights):
+    n_tensor = len(parts)
+    rows, width = parts[0].shape
+    depth, hidden = weights[0].shape[1:]
+    first = hidden // 3 // 128 * 128
+    blocks = (first, hidden - first)
+    hbm = pl.BlockSpec(memory_space=pltpu.HBM)
+    hidden_rows, own_down, *others = pl.pallas_call(
+        functools.partial(others_kernel, n_tensor, blocks),
+        out_shape=[jax.ShapeDtypeStruct((rows, hidden), BF16), jax.ShapeDtypeStruct((hidden, width), BF16)]
+        + [jax.ShapeDtypeStruct((rows, width), BF16) for _ in parts[1:]],
+        in_specs=[pl.BlockSpec(memory_space=pltpu.SMEM)] + [vmem() for _ in parts] + [hbm, hbm, hbm],
+        out_specs=[vmem() for _ in range(1 + n_tensor)],
+        scratch_shapes=[
+            pltpu.VMEM((depth, hidden), BF16),
+            pltpu.VMEM((depth, hidden), BF16),
+            pltpu.VMEM((max(n_tensor - 1, 1), hidden, width), BF16),
+            pltpu.VMEM((rows, depth), BF16),
+            pltpu.SemaphoreType.DMA((2 * len(blocks) + n_tensor,)),
+        ],
+        compiler_params=params(36),
+        cost_estimate=pl.CostEstimate(
+            flops=4 * rows * depth * hidden + 2 * rows * (depth - width) * hidden,
+            bytes_accessed=6 * depth * hidden,
+            transcendentals=rows * hidden,
+        ),
+        name="other_shares",
+    )(where, *parts, *[in_hbm(weight) for weight in weights])
+    return hidden_rows, own_down, others
+
+
+def own_share_kernel(hidden_ref, down_ref, out_ref):
+    out_ref[...] = jnp.dot(hidden_ref[...], down_ref[...], preferred_element_type=F32).astype(BF16)
+
+
+def own_share(hidden_rows, own_down):
+    rows, hidden = hidden_rows.shape
+    width = own_down.shape[1]
+    return pl.pallas_call(
+        own_share_kernel,
+        out_shape=jax.ShapeDtypeStruct((rows, width), BF16),
+        in_specs=[vmem(), vmem()],
+        out_specs=vmem(),
+        compiler_params=params(16),
+        cost_estimate=pl.CostEstimate(
+            flops=2 * rows * width * hidden, bytes_accessed=2 * hidden * (rows + width), transcendentals=0
+        ),
+        name="own_share",
+    )(hidden_rows, own_down)
+
+
 def row_cuts(rows):
     cut = rows // 4 if rows % 64 == 0 else rows
     return [pl.ds(low, cut) for low in range(0, rows, cut)]
@@ -304,11 +407,17 @@
     maps = combine_map(expert_ids, n_expert, chunks)
     weights = (gate_weight, up_weight, down_weight)
     backs = []
-    for rows in outgoing:
+    for index, rows in enumerate(outgoing):
         arrived = exchange(rows, n_expert)
         parts = [arrived] + [shifted(arrived, shift) for shift in range(1, n_tensor)]
-        shares = expert_rows(where, parts, weights)
-        total = add([shares[0]] + [shifted(shares[shift], -shift) for shift in range(1, n_tensor)])
+        if index < len(outgoing) - 1:
+            own, *others = expert_rows(where, parts, weights)
+            received = [shifted(share, -shift) for shift, share in enumerate(others, 1)]
+        else:
+            hidden_rows, own_down, others = other_shares(where, parts, weights)
+            received = [shifted(share, -shift) for shift, share in enumerate(others, 1)]
+            own = own_share(hidden_rows, own_down)
+        total = add([own] + received)
         backs.append(exchange(total, n_expert))
     picked = [pick(pick_map, back) for pick_map, back in zip(maps[:-1], backs[:-1])]
     return finish(maps[-1], backs[-1], gate_scale, picked)

time: 84.3 us -> 83 us (0.985)
  waiting for transfers between devices: 12.2 us -> 10.6 us
    pallas_call x0 -> x2, Pallas kernels: none -> 12.8 us  [the longest x1 11 us: other_shares(): pl.pallas_call(functools.partial(others_kernel, n_tensor, blocks), out_sh...]
    pallas_call x2 -> x1, Pallas kernels: 25.1 us -> 12.6 us  [expert_rows(): pl.pallas_call(functools.partial(expert_kernel, n_tensor, blocks), out_sh...]
    ppermute x4, waiting for transfers between devices: 3.3 us -> 1.51 us  [shifted(): lax.ppermute(rows, 'tensor', [(i, (i - shift) % n_tensor) for i in range(...]
  transfers between devices with their start and end apart: 7 -> 7, of which waited for: 3 -> 3; matrix products, arithmetic and copies ran while one was open for 0% -> 0% of each run, Pallas kernels for 34% -> 35%
where the time goes in v4:
time: 83 us; the launch traced here: 82.5 us
  Pallas kernels  32.2 us (39%)
  blocking collectives  19.5 us (23%)
  starting transfers between devices  19.5 us (23%)
  waiting for transfers between devices  10.6 us (13%)
    all_to_all x1, blocking collectives, exchange(): lax.all_to_all(rows.reshape(n_expert, size, -1), 'expert', split_axis=0,...  19.5 us
    all_to_all x3, starting transfers between devices, exchange(): lax.all_to_all(rows.reshape(n_expert, size, -1), 'expert', split_axis=0,...  18.9 us
    pallas_call x1, Pallas kernels, expert_rows(): pl.pallas_call(functools.partial(expert_kernel, n_tensor, blocks), out_sh...  12.6 us
    pallas_call x1, Pallas kernels, other_shares(): pl.pallas_call(functools.partial(others_kernel, n_tensor, blocks), out_sh...  11 us
    all_to_all x3, waiting for transfers between devices, exchange(): lax.all_to_all(rows.reshape(n_expert, size, -1), 'expert', split_axis=0,...  9.11 us
    pallas_call x1, Pallas kernels, dispatch(): pl.pallas_call(functools.partial(dispatch_kernel, n_expert, chunks), out_...  2.4 us
    pallas_call x1, Pallas kernels, own_share(): pl.pallas_call(own_share_kernel, out_shape=jax.ShapeDtypeStruct((rows, wi...  1.78 us
    pallas_call x2, Pallas kernels, add(): pl.pallas_call(add_kernel, out_shape=jax.ShapeDtypeStruct(shape, BF16), i...  1.71 us
  transfers between devices with their start and end apart: 7, of which 3 were waited for; matrix products, arithmetic and copies ran while one was open for 0% of the time, Pallas kernels for 35%

profile of v4, /device:TPU:0, one launch (start us, length us, event | category | flops | bytes accessed | tf_op | source)
XLA Modules:
  0.0 82.5 jit_solution(3968722837509422299)
XLA Ops:
  0.0 2.4 %dispatch.1 = (bf16[512,512]{1,0:T(8,128)(2,1)S(1)}, bf16[512,512]{1,0:T(8,128)(2,1)}) custom-call(s32[1,512]{1,0:T(1,128)} %bitcast.19, bf16[512,512]{1,0:T(8,128)(2,1)} %tok_hbm.1), custom_call_target="tpu_custom_call" | custom-call | tf_op jit(solution)/shard_map/dispatch/pallas_call | solution.py:92
  2.4 19.5 %all_to_all.20 = bf16[16,32,512]{2,1,0:T(8,128)(2,1)S(1)} all-to-all(bf16[16,32,512]{2,1,0:T(8,128)(2,1)S(1)} %bitcast.18), channel_id=1, replica_groups={{20,8,18,16,10,12,22,0,24,14,26,28,2,4,30,6},{21,9,19,17,11,13,23,1,25,..., dimensions={0} | all-to-all | bytes 1048576 | tf_op jit(solution)/shard_map/all_to_all | solution.py:386
  21.9 0.0 collective-permute-start.2
  21.9 6.8 %all-to-all-start = ((bf16[16,32,512]{2,1,0:T(8,128)(2,1)}), bf16[16,32,512]{2,1,0:T(8,128)(2,1)S(1)}, u32[]{:S(2)}, u32[]{:S(2)}) async-start(bf16[16,32,512]{2,1,0:T(8,128)(2,1)} %bitcast.3), calls=%async_computation | async-start | bytes 1048576 | tf_op jit(solution)/shard_map/all_to_all | solution.py:386
  28.8 0.0 collective-permute-done.2.refs_1_
  28.8 12.6 %expert_rows.1 = (bf16[512,512]{1,0:T(8,128)(2,1)S(1)}, bf16[512,512]{1,0:T(8,128)(2,1)S(1)}) custom-call(s32[1]{0:T(128)} %bitcast.1.where_ref, bf16[512,512]{1,0:T(8,128)(2,1)S(1)} %bitcast.17, bf16[512,512]{1,0:T(8,128)(2,1)S(1)} %collective-permute-done.2.refs_1_, bf16[1,1024,3072]{2,1,0:T(8,128)(2,1)} %refs_2_.3, bf16[1,1024,3072]{2,1,0:T(8,128)(2,1)} %refs_3_.3, ...), custom_call_target="tpu_custom_call" | custom-call | flops 9663676416 | bytes 18874368 | tf_op jit(solution)/shard_map/expert_rows/pallas_call | solution.py:228
  41.4 0.1 collective-permute-start.3
  41.4 0.0 all-to-all-done
  41.5 0.5 collective-permute-start
  41.9 1.4 %collective-permute-done.3.refs_1_ = bf16[512,512]{1,0:T(8,128)(2,1)S(1)} collective-permute-done((bf16[512,512]{1,0:T(8,128)(2,1)S(1)}, bf16[512,512]{1,0:T(8,128)(2,1)S(1)}, u32[]{:S(2)}, u32[]{:S(2)}) %collective-permute-start.3) | collective-permute-done | bytes 524320 | tf_op jit(solution)/shard_map/ppermute | solution.py:404
  43.3 0.9 %add_shares.3 = bf16[512,512]{1,0:T(8,128)(2,1)} custom-call(bf16[512,512]{1,0:T(8,128)(2,1)S(1)} %get-tuple-element.21.refs_0_, bf16[512,512]{1,0:T(8,128)(2,1)S(1)} %collective-permute-done.3.refs_1_), custom_call_target="tpu_custom_call" | custom-call | tf_op jit(solution)/shard_map/add_shares/pallas_call | solution.py:373
  44.2 6.0 %all-to-all-start.3 = ((bf16[16,32,512]{2,1,0:T(8,128)(2,1)}), bf16[16,32,512]{2,1,0:T(8,128)(2,1)S(1)}, u32[]{:S(2)}, u32[]{:S(2)}) async-start(bf16[16,32,512]{2,1,0:T(8,128)(2,1)} %bitcast.10), calls=%async_computation.3 | async-start | bytes 1048576 | tf_op jit(solution)/shard_map/all_to_all | solution.py:386
  50.2 0.0 collective-permute-done.refs_1_
  50.2 11.0 %other_shares.1 = (bf16[512,3072]{1,0:T(8,128)(2,1)S(1)}, bf16[3072,512]{1,0:T(8,128)(2,1)S(1)}, bf16[512,512]{1,0:T(8,128)(2,1)S(1)}) custom-call(s32[1]{0:T(128)} %bitcast.1.where_ref, bf16[512,512]{1,0:T(8,128)(2,1)S(1)} %bitcast.15, bf16[512,512]{1,0:T(8,128)(2,1)S(1)} %collective-permute-done.refs_1_, bf16[1,1024,3072]{2,1,0:T(8,128)(2,1)} %refs_2_.3, ...), custom_call_target="tpu_custom_call" | custom-call | flops 8053063680 | bytes 18874368 | tf_op jit(solution)/shard_map/other_shares/pallas_call | solution.py:308
  61.3 0.0 copy-start
  61.3 0.0 copy-start.1
  61.3 0.1 collective-permute-start.1
  61.4 1.8 %own_share.1.refs_0_ = bf16[512,512]{1,0:T(8,128)(2,1)S(1)} custom-call(bf16[512,3072]{1,0:T(8,128)(2,1)S(1)} %get-tuple-element.16.hidden_ref, bf16[3072,512]{1,0:T(8,128)(2,1)S(1)} %get-tuple-element.17.down_ref), custom_call_target="tpu_custom_call" | custom-call | flops 1610612736 | bytes 6291456 | tf_op jit(solution)/shard_map/own_share/pallas_call | solution.py:339
  63.1 0.1 collective-permute-done.1.refs_1_
  63.3 0.8 %add_shares.2 = bf16[512,512]{1,0:T(8,128)(2,1)} custom-call(bf16[512,512]{1,0:T(8,128)(2,1)S(1)} %own_share.1.refs_0_, bf16[512,512]{1,0:T(8,128)(2,1)S(1)} %collective-permute-done.1.refs_1_), custom_call_target="tpu_custom_call" | custom-call | tf_op jit(solution)/shard_map/add_shares/pallas_call | solution.py:373
  64.1 0.0 all-to-all-done.3
  64.1 6.0 %all-to-all-start.1 = ((bf16[16,32,512]{2,1,0:T(8,128)(2,1)}), bf16[16,32,512]{2,1,0:T(8,128)(2,1)S(1)}, u32[]{:S(2)}, u32[]{:S(2)}) async-start(bf16[16,32,512]{2,1,0:T(8,128)(2,1)} %bitcast.5), calls=%async_computation.1 | async-start | bytes 1048576 | tf_op jit(solution)/shard_map/all_to_all | solution.py:386
  70.2 0.0 copy-done
  70.2 0.1 copy.7.ids_ref
  70.3 1.1 %combine_map.1 = (bf16[512,512]{1,0:T(8,128)(2,1)S(1)}, bf16[512,512]{1,0:T(8,128)(2,1)S(1)}) custom-call(s32[512,1]{1,0:T(8,128)S(1)} %copy.7.ids_ref), custom_call_target="tpu_custom_call" | custom-call | tf_op jit(solution)/shard_map/combine_map/pallas_call | solution.py:124
  71.5 0.0 copy-done.1
  71.5 0.1 copy.8.scale_ref
  71.6 0.4 pick.1.refs_0_
  72.1 9.1 %all-to-all-done.1 = bf16[16,32,512]{2,1,0:T(8,128)(2,1)S(1)} async-done(((bf16[16,32,512]{2,1,0:T(8,128)(2,1)}), bf16[16,32,512]{2,1,0:T(8,128)(2,1)S(1)}, u32[]{:S(2)}, u32[]{:S(2)}) %all-to-all-start.1) | async-done | bytes 524320 | tf_op jit(solution)/shard_map/all_to_all | solution.py:386
  81.2 1.1 %finish.1 = bf16[512,512]{1,0:T(8,128)(2,1)} custom-call(bf16[512,512]{1,0:T(8,128)(2,1)S(1)} %get-tuple-element.14.map_ref, bf16[512,512]{1,0:T(8,128)(2,1)S(1)} %bitcast.13, f32[512,1]{1,0:T(8,128)S(1)} %copy.8.scale_ref, bf16[512,512]{1,0:T(8,128)(2,1)S(1)} %pick.1.refs_0_), custom_call_target="tpu_custom_call" | custom-call | tf_op jit(solution)/shard_map/finish/pallas_call | solution.py:167
Async XLA Ops:
  21.9 6.8 %collective-permute-start.2 = (bf16[512,512]{1,0:T(8,128)(2,1)S(1)}, bf16[512,512]{1,0:T(8,128)(2,1)S(1)}, u32[]{:S(2)}, u32[]{:S(2)}) collective-permute-start(bf16[512,512]{1,0:T(8,128)(2,1)S(1)} %bitcast.16), channel_id=1, source_target_pairs={{0,1},{1,0},{2,3},{3,2},{4,5},{5,4},{6,7},{7,6},{8,9},{9,8},{10,11... | collective-permute-start | bytes 1572872 | tf_op jit(solution)/shard_map/ppermute | solution.py:404
  21.9 19.5 %all-to-all-start = ((bf16[16,32,512]{2,1,0:T(8,128)(2,1)}), bf16[16,32,512]{2,1,0:T(8,128)(2,1)S(1)}, u32[]{:S(2)}, u32[]{:S(2)}) async-start(bf16[16,32,512]{2,1,0:T(8,128)(2,1)} %bitcast.3), calls=%async_computation | async-start | bytes 1048576 | tf_op jit(solution)/shard_map/all_to_all | solution.py:386
  41.4 2.0 %collective-permute-start.3 = (bf16[512,512]{1,0:T(8,128)(2,1)S(1)}, bf16[512,512]{1,0:T(8,128)(2,1)S(1)}, u32[]{:S(2)}, u32[]{:S(2)}) collective-permute-start(bf16[512,512]{1,0:T(8,128)(2,1)S(1)} %get-tuple-element.22), channel_id=1, source_target_pairs={{0,1},{1,0},{2,3},{3,2},{4,5},{5,4},{6,7},{7,6},{8,9},{9,8},{10,11... | collective-permute-start | bytes 1572872 | tf_op jit(solution)/shard_map/ppermute | solution.py:404
  41.5 8.8 %collective-permute-start = (bf16[512,512]{1,0:T(8,128)(2,1)S(1)}, bf16[512,512]{1,0:T(8,128)(2,1)S(1)}, u32[]{:S(2)}, u32[]{:S(2)}) collective-permute-start(bf16[512,512]{1,0:T(8,128)(2,1)S(1)} %bitcast.14), channel_id=1, source_target_pairs={{0,1},{1,0},{2,3},{3,2},{4,5},{5,4},{6,7},{7,6},{8,9},{9,8},{10,11... | collective-permute-start | bytes 1572872 | tf_op jit(solution)/shard_map/ppermute | solution.py:404
  44.2 19.9 %all-to-all-start.3 = ((bf16[16,32,512]{2,1,0:T(8,128)(2,1)}), bf16[16,32,512]{2,1,0:T(8,128)(2,1)S(1)}, u32[]{:S(2)}, u32[]{:S(2)}) async-start(bf16[16,32,512]{2,1,0:T(8,128)(2,1)} %bitcast.10), calls=%async_computation.3 | async-start | bytes 1048576 | tf_op jit(solution)/shard_map/all_to_all | solution.py:386
  61.3 8.9 %copy-start = (s32[512]{0:T(512)S(1)}, s32[512]{0:T(512)}, u32[]{:S(2)}) copy-start(s32[512]{0:T(512)} %param.7) | copy-start | bytes 6148
  61.3 10.2 %copy-start.1 = (f32[512]{0:T(512)S(1)}, f32[512]{0:T(512)}, u32[]{:S(2)}) copy-start(f32[512]{0:T(512)} %param.8) | copy-start | bytes 6148
  61.3 2.0 %collective-permute-start.1 = (bf16[512,512]{1,0:T(8,128)(2,1)S(1)}, bf16[512,512]{1,0:T(8,128)(2,1)S(1)}, u32[]{:S(2)}, u32[]{:S(2)}) collective-permute-start(bf16[512,512]{1,0:T(8,128)(2,1)S(1)} %get-tuple-element.18), channel_id=1, source_target_pairs={{0,1},{1,0},{2,3},{3,2},{4,5},{5,4},{6,7},{7,6},{8,9},{9,8},{10,11... | collective-permute-start | bytes 1572872 | tf_op jit(solution)/shard_map/ppermute | solution.py:404
  64.1 17.1 %all-to-all-start.1 = ((bf16[16,32,512]{2,1,0:T(8,128)(2,1)}), bf16[16,32,512]{2,1,0:T(8,128)(2,1)S(1)}, u32[]{:S(2)}, u32[]{:S(2)}) async-start(bf16[16,32,512]{2,1,0:T(8,128)(2,1)} %bitcast.5), calls=%async_computation.1 | async-start | bytes 1048576 | tf_op jit(solution)/shard_map/all_to_all | solution.py:386

commit v5 on v4

--- a/solution.py
+++ b/solution.py
@@ -350,7 +350,7 @@
 
 
 def row_cuts(rows):
-    cut = rows // 4 if rows % 64 == 0 else rows
+    cut = rows // 2 if rows % 32 == 0 else rows
     return [pl.ds(low, cut) for low in range(0, rows, cut)]
 
 

time: 83 us -> 83 us (level)
  no operation moved by 1% of the time
where the time goes in v5:
time: 83 us; the launch traced here: 82.5 us
  Pallas kernels  32.2 us (39%)
  blocking collectives  19.5 us (23%)
  starting transfers between devices  19.5 us (23%)
  waiting for transfers between devices  10.6 us (13%)
    all_to_all x1, blocking collectives, exchange(): lax.all_to_all(rows.reshape(n_expert, size, -1), 'expert', split_axis=0,...  19.5 us
    all_to_all x3, starting transfers between devices, exchange(): lax.all_to_all(rows.reshape(n_expert, size, -1), 'expert', split_axis=0,...  18.9 us
    pallas_call x1, Pallas kernels, expert_rows(): pl.pallas_call(functools.partial(expert_kernel, n_tensor, blocks), out_sh...  12.6 us
    pallas_call x1, Pallas kernels, other_shares(): pl.pallas_call(functools.partial(others_kernel, n_tensor, blocks), out_sh...  11 us
    all_to_all x3, waiting for transfers between devices, exchange(): lax.all_to_all(rows.reshape(n_expert, size, -1), 'expert', split_axis=0,...  9.11 us
    pallas_call x1, Pallas kernels, dispatch(): pl.pallas_call(functools.partial(dispatch_kernel, n_expert, chunks), out_...  2.4 us
    pallas_call x1, Pallas kernels, own_share(): pl.pallas_call(own_share_kernel, out_shape=jax.ShapeDtypeStruct((rows, wi...  1.78 us
    pallas_call x2, Pallas kernels, add(): pl.pallas_call(add_kernel, out_shape=jax.ShapeDtypeStruct(shape, BF16), i...  1.73 us
  transfers between devices with their start and end apart: 7, of which 3 were waited for; matrix products, arithmetic and copies ran while one was open for 0% of the time, Pallas kernels for 35%

profile of v5, /device:TPU:0, one launch (start us, length us, event | category | flops | bytes accessed | tf_op | source)
XLA Modules:
  0.0 82.5 jit_solution(3365898759670948521)
XLA Ops:
  0.0 2.4 %dispatch.1 = (bf16[512,512]{1,0:T(8,128)(2,1)S(1)}, bf16[512,512]{1,0:T(8,128)(2,1)}) custom-call(s32[1,512]{1,0:T(1,128)} %bitcast.19, bf16[512,512]{1,0:T(8,128)(2,1)} %tok_hbm.1), custom_call_target="tpu_custom_call" | custom-call | tf_op jit(solution)/shard_map/dispatch/pallas_call | solution.py:92
  2.4 19.5 %all_to_all.20 = bf16[16,32,512]{2,1,0:T(8,128)(2,1)S(1)} all-to-all(bf16[16,32,512]{2,1,0:T(8,128)(2,1)S(1)} %bitcast.18), channel_id=1, replica_groups={{20,8,18,16,10,12,22,0,24,14,26,28,2,4,30,6},{21,9,19,17,11,13,23,1,25,..., dimensions={0} | all-to-all | bytes 1048576 | tf_op jit(solution)/shard_map/all_to_all | solution.py:386
  21.9 0.0 collective-permute-start.2
  21.9 6.8 %all-to-all-start = ((bf16[16,32,512]{2,1,0:T(8,128)(2,1)}), bf16[16,32,512]{2,1,0:T(8,128)(2,1)S(1)}, u32[]{:S(2)}, u32[]{:S(2)}) async-start(bf16[16,32,512]{2,1,0:T(8,128)(2,1)} %bitcast.3), calls=%async_computation | async-start | bytes 1048576 | tf_op jit(solution)/shard_map/all_to_all | solution.py:386
  28.8 0.0 collective-permute-done.2.refs_1_
  28.8 12.6 %expert_rows.1 = (bf16[512,512]{1,0:T(8,128)(2,1)S(1)}, bf16[512,512]{1,0:T(8,128)(2,1)S(1)}) custom-call(s32[1]{0:T(128)} %bitcast.1.where_ref, bf16[512,512]{1,0:T(8,128)(2,1)S(1)} %bitcast.17, bf16[512,512]{1,0:T(8,128)(2,1)S(1)} %collective-permute-done.2.refs_1_, bf16[1,1024,3072]{2,1,0:T(8,128)(2,1)} %refs_2_.3, bf16[1,1024,3072]{2,1,0:T(8,128)(2,1)} %refs_3_.3, ...), custom_call_target="tpu_custom_call" | custom-call | flops 9663676416 | bytes 18874368 | tf_op jit(solution)/shard_map/expert_rows/pallas_call | solution.py:228
  41.4 0.1 collective-permute-start.3
  41.4 0.0 all-to-all-done
  41.5 0.5 collective-permute-start
  41.9 1.4 %collective-permute-done.3.refs_1_ = bf16[512,512]{1,0:T(8,128)(2,1)S(1)} collective-permute-done((bf16[512,512]{1,0:T(8,128)(2,1)S(1)}, bf16[512,512]{1,0:T(8,128)(2,1)S(1)}, u32[]{:S(2)}, u32[]{:S(2)}) %collective-permute-start.3) | collective-permute-done | bytes 524320 | tf_op jit(solution)/shard_map/ppermute | solution.py:404
  43.3 0.9 %add_shares.3 = bf16[512,512]{1,0:T(8,128)(2,1)} custom-call(bf16[512,512]{1,0:T(8,128)(2,1)S(1)} %get-tuple-element.21.refs_0_, bf16[512,512]{1,0:T(8,128)(2,1)S(1)} %collective-permute-done.3.refs_1_), custom_call_target="tpu_custom_call" | custom-call | tf_op jit(solution)/shard_map/add_shares/pallas_call | solution.py:373
  44.2 6.0 %all-to-all-start.3 = ((bf16[16,32,512]{2,1,0:T(8,128)(2,1)}), bf16[16,32,512]{2,1,0:T(8,128)(2,1)S(1)}, u32[]{:S(2)}, u32[]{:S(2)}) async-start(bf16[16,32,512]{2,1,0:T(8,128)(2,1)} %bitcast.10), calls=%async_computation.3 | async-start | bytes 1048576 | tf_op jit(solution)/shard_map/all_to_all | solution.py:386
  50.2 0.0 collective-permute-done.refs_1_
  50.3 11.0 %other_shares.1 = (bf16[512,3072]{1,0:T(8,128)(2,1)S(1)}, bf16[3072,512]{1,0:T(8,128)(2,1)S(1)}, bf16[512,512]{1,0:T(8,128)(2,1)S(1)}) custom-call(s32[1]{0:T(128)} %bitcast.1.where_ref, bf16[512,512]{1,0:T(8,128)(2,1)S(1)} %bitcast.15, bf16[512,512]{1,0:T(8,128)(2,1)S(1)} %collective-permute-done.refs_1_, bf16[1,1024,3072]{2,1,0:T(8,128)(2,1)} %refs_2_.3, ...), custom_call_target="tpu_custom_call" | custom-call | flops 8053063680 | bytes 18874368 | tf_op jit(solution)/shard_map/other_shares/pallas_call | solution.py:308
  61.3 0.0 copy-start
  61.3 0.0 copy-start.1
  61.3 0.1 collective-permute-start.1
  61.4 1.8 %own_share.1.refs_0_ = bf16[512,512]{1,0:T(8,128)(2,1)S(1)} custom-call(bf16[512,3072]{1,0:T(8,128)(2,1)S(1)} %get-tuple-element.16.hidden_ref, bf16[3072,512]{1,0:T(8,128)(2,1)S(1)} %get-tuple-element.17.down_ref), custom_call_target="tpu_custom_call" | custom-call | flops 1610612736 | bytes 6291456 | tf_op jit(solution)/shard_map/own_share/pallas_call | solution.py:339
  63.2 0.1 collective-permute-done.1.refs_1_
  63.3 0.9 %add_shares.2 = bf16[512,512]{1,0:T(8,128)(2,1)} custom-call(bf16[512,512]{1,0:T(8,128)(2,1)S(1)} %own_share.1.refs_0_, bf16[512,512]{1,0:T(8,128)(2,1)S(1)} %collective-permute-done.1.refs_1_), custom_call_target="tpu_custom_call" | custom-call | tf_op jit(solution)/shard_map/add_shares/pallas_call | solution.py:373
  64.2 0.0 all-to-all-done.3
  64.2 6.0 %all-to-all-start.1 = ((bf16[16,32,512]{2,1,0:T(8,128)(2,1)}), bf16[16,32,512]{2,1,0:T(8,128)(2,1)S(1)}, u32[]{:S(2)}, u32[]{:S(2)}) async-start(bf16[16,32,512]{2,1,0:T(8,128)(2,1)} %bitcast.5), calls=%async_computation.1 | async-start | bytes 1048576 | tf_op jit(solution)/shard_map/all_to_all | solution.py:386
  70.2 0.0 copy-done
  70.2 0.1 copy.7.ids_ref
  70.3 1.1 %combine_map.1 = (bf16[512,512]{1,0:T(8,128)(2,1)S(1)}, bf16[512,512]{1,0:T(8,128)(2,1)S(1)}) custom-call(s32[512,1]{1,0:T(8,128)S(1)} %copy.7.ids_ref), custom_call_target="tpu_custom_call" | custom-call | tf_op jit(solution)/shard_map/combine_map/pallas_call | solution.py:124
  71.5 0.0 copy-done.1
  71.5 0.1 copy.8.scale_ref
  71.6 0.4 pick.1.refs_0_
  72.1 9.1 %all-to-all-done.1 = bf16[16,32,512]{2,1,0:T(8,128)(2,1)S(1)} async-done(((bf16[16,32,512]{2,1,0:T(8,128)(2,1)}), bf16[16,32,512]{2,1,0:T(8,128)(2,1)S(1)}, u32[]{:S(2)}, u32[]{:S(2)}) %all-to-all-start.1) | async-done | bytes 524320 | tf_op jit(solution)/shard_map/all_to_all | solution.py:386
  81.2 1.2 %finish.1 = bf16[512,512]{1,0:T(8,128)(2,1)} custom-call(bf16[512,512]{1,0:T(8,128)(2,1)S(1)} %get-tuple-element.14.map_ref, bf16[512,512]{1,0:T(8,128)(2,1)S(1)} %bitcast.13, f32[512,1]{1,0:T(8,128)S(1)} %copy.8.scale_ref, bf16[512,512]{1,0:T(8,128)(2,1)S(1)} %pick.1.refs_0_), custom_call_target="tpu_custom_call" | custom-call | tf_op jit(solution)/shard_map/finish/pallas_call | solution.py:167
Async XLA Ops:
  21.9 6.8 %collective-permute-start.2 = (bf16[512,512]{1,0:T(8,128)(2,1)S(1)}, bf16[512,512]{1,0:T(8,128)(2,1)S(1)}, u32[]{:S(2)}, u32[]{:S(2)}) collective-permute-start(bf16[512,512]{1,0:T(8,128)(2,1)S(1)} %bitcast.16), channel_id=1, source_target_pairs={{0,1},{1,0},{2,3},{3,2},{4,5},{5,4},{6,7},{7,6},{8,9},{9,8},{10,11... | collective-permute-start | bytes 1572872 | tf_op jit(solution)/shard_map/ppermute | solution.py:404
  21.9 19.5 %all-to-all-start = ((bf16[16,32,512]{2,1,0:T(8,128)(2,1)}), bf16[16,32,512]{2,1,0:T(8,128)(2,1)S(1)}, u32[]{:S(2)}, u32[]{:S(2)}) async-start(bf16[16,32,512]{2,1,0:T(8,128)(2,1)} %bitcast.3), calls=%async_computation | async-start | bytes 1048576 | tf_op jit(solution)/shard_map/all_to_all | solution.py:386
  41.4 2.0 %collective-permute-start.3 = (bf16[512,512]{1,0:T(8,128)(2,1)S(1)}, bf16[512,512]{1,0:T(8,128)(2,1)S(1)}, u32[]{:S(2)}, u32[]{:S(2)}) collective-permute-start(bf16[512,512]{1,0:T(8,128)(2,1)S(1)} %get-tuple-element.22), channel_id=1, source_target_pairs={{0,1},{1,0},{2,3},{3,2},{4,5},{5,4},{6,7},{7,6},{8,9},{9,8},{10,11... | collective-permute-start | bytes 1572872 | tf_op jit(solution)/shard_map/ppermute | solution.py:404
  41.5 8.8 %collective-permute-start = (bf16[512,512]{1,0:T(8,128)(2,1)S(1)}, bf16[512,512]{1,0:T(8,128)(2,1)S(1)}, u32[]{:S(2)}, u32[]{:S(2)}) collective-permute-start(bf16[512,512]{1,0:T(8,128)(2,1)S(1)} %bitcast.14), channel_id=1, source_target_pairs={{0,1},{1,0},{2,3},{3,2},{4,5},{5,4},{6,7},{7,6},{8,9},{9,8},{10,11... | collective-permute-start | bytes 1572872 | tf_op jit(solution)/shard_map/ppermute | solution.py:404
  44.2 19.9 %all-to-all-start.3 = ((bf16[16,32,512]{2,1,0:T(8,128)(2,1)}), bf16[16,32,512]{2,1,0:T(8,128)(2,1)S(1)}, u32[]{:S(2)}, u32[]{:S(2)}) async-start(bf16[16,32,512]{2,1,0:T(8,128)(2,1)} %bitcast.10), calls=%async_computation.3 | async-start | bytes 1048576 | tf_op jit(solution)/shard_map/all_to_all | solution.py:386
  61.3 8.9 %copy-start = (s32[512]{0:T(512)S(1)}, s32[512]{0:T(512)}, u32[]{:S(2)}) copy-start(s32[512]{0:T(512)} %param.7) | copy-start | bytes 6148
  61.3 10.2 %copy-start.1 = (f32[512]{0:T(512)S(1)}, f32[512]{0:T(512)}, u32[]{:S(2)}) copy-start(f32[512]{0:T(512)} %param.8) | copy-start | bytes 6148
  61.3 2.0 %collective-permute-start.1 = (bf16[512,512]{1,0:T(8,128)(2,1)S(1)}, bf16[512,512]{1,0:T(8,128)(2,1)S(1)}, u32[]{:S(2)}, u32[]{:S(2)}) collective-permute-start(bf16[512,512]{1,0:T(8,128)(2,1)S(1)} %get-tuple-element.18), channel_id=1, source_target_pairs={{0,1},{1,0},{2,3},{3,2},{4,5},{5,4},{6,7},{7,6},{8,9},{9,8},{10,11... | collective-permute-start | bytes 1572872 | tf_op jit(solution)/shard_map/ppermute | solution.py:404
  64.2 17.0 %all-to-all-start.1 = ((bf16[16,32,512]{2,1,0:T(8,128)(2,1)}), bf16[16,32,512]{2,1,0:T(8,128)(2,1)S(1)}, u32[]{:S(2)}, u32[]{:S(2)}) async-start(bf16[16,32,512]{2,1,0:T(8,128)(2,1)} %bitcast.5), calls=%async_computation.1 | async-start | bytes 1048576 | tf_op jit(solution)/shard_map/all_to_all | solution.py:386
